TPU v7x, 128 devices: a whole 4x4x4 slice. The times are simulated.
128 devices in a mesh: fx: 8 (over z, core), fy: 16 (over x, y).
Axes of the slice: x: 4, y: 4, z: 4, core: 2. Of those that a mesh axis runs over, the one named last changes fastest.
Arguments:
- tracers: float32 [8, 72, 128, 2048], P(None, None, 'fx', 'fy'), may hold values from -6 to 6
- group_dest: int32 [128, 2048], P('fx', 'fy'), may hold values from 0 to 127, as said below
- group_slot: int32 [128, 2048], P('fx', 'fy'), may hold values from 0 to 2047, as said below
- diffusivity: float32 [72, 262144], P(None, ('fx', 'fy')), may hold values from 0.05 to 5
- surface_flux: float32 [8, 262144], P(None, ('fx', 'fy')), may hold values from -6 to 6
Outputs:
- tracers_out: float32 [8, 72, 128, 2048], P(None, None, 'fx', 'fy')
Inputs may be any that keep to these rules, and one draw needn't show every extreme that they name: `group_dest`: on every device exactly 512 columns name another device and every device is named by exactly 512 columns of other devices; at most 6 columns of one device name one other device, exactly 6 for some pairs; the number of columns of device r that name device (r + o) mod 128 depends on o only. `group_slot`: together with group_dest it names every physics slot of all devices exactly once.
All inputs are finite; a program needn't handle non-finite values.
Results may differ from a plain program's by a relative error of at most 0.00002.
Values sent between devices are 32-bit elements; how exact they have to be, the bound alone decides.
A program may use at most 128 MiB of HBM per device.

v0:
```python
import jax
import jax.numpy as jnp
from jax import lax
from jax.sharding import PartitionSpec as P

hyper_rate = 0.025


def with_halo(cells, sides, width):
    for axis, dim in sides:
        count = lax.axis_size(axis)
        head = lax.slice_in_dim(cells, 0, width, axis=dim)
        tail = lax.slice_in_dim(cells, cells.shape[dim] - width, cells.shape[dim], axis=dim)
        cells = jnp.concatenate(
            [
                lax.ppermute(tail, axis, [(i, (i + 1) % count) for i in range(count)]),
                cells,
                lax.ppermute(head, axis, [((i + 1) % count, i) for i in range(count)]),
            ],
            axis=dim,
        )
    return cells


def column_solve(columns, column_kv, column_flux):
    level_count = column_kv.shape[0]
    ratios = []
    partials = []
    ratio_prev = jnp.zeros_like(column_kv[0])
    partial_prev = jnp.zeros_like(columns[:, 0])
    for level in range(level_count):
        above_rate = column_kv[level - 1] if level >= 1 else jnp.zeros_like(column_kv[0])
        below_rate = column_kv[level] if level <= level_count - 2 else jnp.zeros_like(column_kv[0])
        middle = 1.0 + above_rate + below_rate
        right_side = columns[:, level]
        if level == level_count - 1:
            middle = middle + column_kv[level]
            right_side = right_side + column_flux
        pivot_value = middle - above_rate * ratio_prev
        ratio_prev = below_rate / pivot_value
        partial_prev = (right_side + above_rate[None, :] * partial_prev) / pivot_value[None, :]
        ratios.append(ratio_prev)
        partials.append(partial_prev)
    solved_levels = [None] * level_count
    next_value = jnp.zeros_like(columns[:, 0])
    for level in range(level_count - 1, -1, -1):
        next_value = partials[level] + ratios[level][None, :] * next_value
        solved_levels[level] = next_value
    return jnp.stack(solved_levels, 1) - columns


def trade_pair(values, slots):
    result = (
        lax.all_to_all(values, ("fx", "fy"), split_axis=1, concat_axis=1, tiled=True),
        lax.all_to_all(slots, ("fx", "fy"), split_axis=1, concat_axis=1, tiled=True),
    )
    return result


def trade_one(values):
    result = lax.all_to_all(values, ("fx", "fy"), split_axis=1, concat_axis=1, tiled=True)
    return result


def laplace_padded(padded):
    return (
        padded[:, :, 2:, 1:-1]
        + padded[:, :, :-2, 1:-1]
        + padded[:, :, 1:-1, 2:]
        + padded[:, :, 1:-1, :-2]
        - 4.0 * padded[:, :, 1:-1, 1:-1]
    )


def edge_padded(field):
    return with_halo(field, (("fx", 2), ("fy", 3)), 1)


def local(tracers, group_dest, group_slot, diffusivity, surface_flux):
    tracer_count, level_count, row_count, col_count = tracers.shape
    columns_dev = row_count * col_count
    column_width = tracer_count * level_count
    devices = lax.axis_size(("fx", "fy"))
    own_index = lax.axis_index(("fx", "fy"))
    moved_count = columns_dev // 4
    capacity = (moved_count + devices - 2) // (devices - 1) + 1
    flat_state = tracers.reshape(column_width, columns_dev)
    destination = group_dest.reshape(columns_dev)
    slot_index = group_slot.reshape(columns_dev)
    leaving = destination != own_index
    match = (jnp.arange(devices, dtype=jnp.int32)[:, None] == destination[None, :]) & leaving[
        None, :
    ]
    running = jnp.cumsum(match.astype(jnp.int32), axis=1) - 1
    block_index = jnp.sum(jnp.where(match, running, 0), axis=0)
    position = jnp.where(leaving, destination * capacity + block_index, devices * capacity)
    kept_slot = jnp.where(leaving, columns_dev, slot_index)
    sent_slots = (
        jnp.full((devices * capacity,), columns_dev, jnp.int32)
        .at[position]
        .set(slot_index, mode="drop")
        .reshape(1, devices, capacity)
    )
    out_buffer = (
        jnp.zeros((column_width, devices * capacity), jnp.float32)
        .at[:, position]
        .set(flat_state, mode="drop")
    )
    arrived, arrived_slots = trade_pair(
        out_buffer.reshape(column_width, devices, capacity), sent_slots
    )
    arrived_slots = arrived_slots.reshape(devices * capacity)
    group_state = (
        jnp.zeros((column_width, columns_dev), jnp.float32)
        .at[:, kept_slot]
        .set(flat_state, mode="drop")
    )
    group_state = group_state.at[:, arrived_slots].set(
        arrived.reshape(column_width, devices * capacity), mode="drop"
    )
    group_change = column_solve(
        group_state.reshape(tracer_count, level_count, columns_dev), diffusivity, surface_flux
    ).reshape(column_width, columns_dev)
    reply = jnp.take(group_change, arrived_slots, axis=1, mode="clip")
    returned = trade_one(reply.reshape(column_width, devices, capacity))
    moved_change = jnp.take(
        returned.reshape(column_width, devices * capacity), position, axis=1, mode="clip"
    )
    kept_change = jnp.take(group_change, slot_index, axis=1, mode="clip")
    increment = jnp.where(leaving[None, :], moved_change, kept_change)
    updated = tracers + increment.reshape(tracers.shape)
    smoothed = laplace_padded(edge_padded(laplace_padded(edge_padded(updated))))
    return updated - hyper_rate * smoothed


def solution(mesh):
    placed = (
        P(None, None, "fx", "fy"),
        P("fx", "fy"),
        P("fx", "fy"),
        P(None, ("fx", "fy")),
        P(None, ("fx", "fy")),
    )
    return jax.shard_map(
        local, mesh=mesh, in_specs=placed, out_specs=P(None, None, "fx", "fy"), check_vma=False
    )
```

profile of v0, /device:TPU:1, one launch (start us, length us, event | category | flops | bytes accessed | tf_op | source)
XLA Modules:
  0.0 394.5 jit_solution(9632025086113089258)
XLA Ops:
  2.3 3.4 select_reduce_fusion
  5.8 1.3 bitcast_clamp_fusion
  7.1 8.2 %scatter_custom_fusion.1 = s32[768]{0:T(1024)S(1)} fusion(s32[2048]{0:T(1024)S(1)} %bitcast.1350, s32[2048]{0:T(1024)} %bitcast.1321, s32[]{:T(128)} %constant.18.clone.1), kind=kCustom, calls=%fused_computation.568 | custom fusion | bytes 3584 | tf_op jit(solution)/shard_map/scatter | solution.py:101
  16.1 11.5 %all-to-all-start = ((s32[1,128,6]{2,0,1:T(1,128)}), s32[1,128,6]{2,0,1:T(1,128)S(1)}, u32[]{:S(2)}, u32[]{:S(2)}) async-start(s32[1,128,6]{2,0,1:T(1,128)} %bitcast.7), calls=%async_computation | async-start | bytes 131072 | tf_op jit(solution)/shard_map/all_to_all | solution.py:55
  27.6 2.6 fusion.249
  30.2 2.3 fusion.248
  32.5 6.7 %copy.1123 = f32[72,8,16,128]{3,1,2,0:T(8,128)} copy(f32[72,8,16,128]{3,2,1,0:T(8,128)} %bitcast.1045) | data formatting | bytes 9437184
  39.3 5.8 %copy.350 = f32[576,2048]{0,1:T(8,128)} copy(f32[576,2048]{1,0:T(8,128)} %bitcast.1055) | data formatting | bytes 9437184 | tf_op jit(solution)/shard_map/reshape | solution.py:87
  45.1 10.6 %scatter_custom_fusion.2 = f32[576,768]{0,1:T(8,128)S(1)} fusion(s32[2048]{0:T(1024)S(1)} %bitcast.1351, f32[576,2048]{0,1:T(8,128)} %copy.350, f32[]{:T(128)} %constant.17.clone.1), kind=kCustom, calls=%fused_computation.9 | custom fusion | bytes 6488068 | tf_op jit(solution)/shard_map/scatter | solution.py:107
  55.6 23.5 %scatter_custom_fusion = f32[576,2048]{0,1:T(8,128)} fusion(s32[2048]{0:T(1024)S(1)} %bitcast.1352, f32[576,2048]{0,1:T(8,128)} %copy.350, f32[]{:T(128)} %constant.17.clone.1), kind=kCustom, calls=%fused_computation.11 | custom fusion | bytes 9437188 | tf_op jit(solution)/shard_map/scatter | solution.py:116
  79.2 1.6 reshape.259
  80.8 9.8 %all-to-all-start.1 = ((f32[576,128,6]{0,2,1:T(8,128)}), f32[576,128,6]{0,2,1:T(8,128)S(1)}, u32[]{:S(2)}, u32[]{:S(2)}) async-start(f32[576,128,6]{0,2,1:T(8,128)} %reshape.259), calls=%async_computation.1 | async-start | bytes 5242880 | tf_op jit(solution)/shard_map/all_to_all | solution.py:54
  91.5 2.7 divide_multiply_fusion.43
  94.2 1.6 slice_divide_fusion
  97.5 28.5 %all-to-all-done.1 = f32[576,128,6]{0,2,1:T(8,128)S(1)} async-done(((f32[576,128,6]{0,2,1:T(8,128)}), f32[576,128,6]{0,2,1:T(8,128)S(1)}, u32[]{:S(2)}, u32[]{:S(2)}) %all-to-all-start.1) | async-done | bytes 1769504 | tf_op jit(solution)/shard_map/all_to_all | solution.py:54
  126.0 1.4 reshape.313
  127.4 11.0 %scatter_custom_fusion.3 = f32[576,2048]{0,1:T(8,128)} fusion(f32[576,2048]{0,1:T(8,128)} %scatter_custom_fusion, s32[768]{0:T(1024)S(1)} %fusion.199, f32[576,768]{0,1:T(8,128)} %reshape.313), kind=kCustom, calls=%fused_computation.43 | custom fusion | bytes 6684672 | tf_op jit(solution)/shard_map/scatter | solution.py:118
  138.4 5.7 %copy.355 = f32[576,2048]{1,0:T(8,128)} copy(f32[576,2048]{0,1:T(8,128)} %scatter_custom_fusion.3) | data formatting | bytes 9437184 | tf_op jit(solution)/shard_map/scatter | solution.py:118
  144.3 5.2 %fusion.247 = (f32[8,1,2048]{2,1,0:T(1,128)S(1)}, f32[8,1,2048]{2,1,0:T(1,128)S(1)}, f32[8,1,2048]{2,1,0:T(1,128)S(1)}, f32[8,1,2048]{2,1,0:T(1,128)S(1)}, f32[8...) fusion(f32[8,72,2048]{2,1,0:T(8,128)} %bitcast.1048), kind=kLoop, calls=%fused_computation.620 | loop fusion | bytes 1966080 | tf_op jit(solution)/shard_map/slice | solution.py:35
  149.5 6.5 %fusion.245 = (f32[8,1,2048]{2,1,0:T(1,128)S(1)}, f32[8,1,2048]{2,1,0:T(1,128)S(1)}, f32[8,1,2048]{2,1,0:T(1,128)S(1)}, f32[8,1,2048]{2,1,0:T(1,128)S(1)}, f32[8...) fusion(f32[8,72,2048]{2,1,0:T(8,128)} %bitcast.1049), kind=kLoop, calls=%fused_computation.618 | loop fusion | bytes 2490368 | tf_op jit(solution)/shard_map/slice | solution.py:35
  156.2 6.2 %fusion.244 = (f32[8,1,2048]{2,1,0:T(1,128)S(1)}, f32[8,1,2048]{2,1,0:T(1,128)S(1)}, f32[8,1,2048]{2,1,0:T(1,128)S(1)}, f32[8,1,2048]{2,1,0:T(1,128)S(1)}, f32[8...) fusion(f32[8,72,2048]{2,1,0:T(8,128)} %bitcast.1050), kind=kLoop, calls=%fused_computation.617 | loop fusion | bytes 2490368 | tf_op jit(solution)/shard_map/slice | solution.py:35
  162.4 6.0 %fusion.246 = (f32[8,1,2048]{2,1,0:T(1,128)S(1)}, f32[8,1,2048]{2,1,0:T(1,128)S(1)}, f32[8,1,2048]{2,1,0:T(1,128)S(1)}, f32[8,1,2048]{2,1,0:T(1,128)S(1)}, f32[8...) fusion(f32[8,72,2048]{2,1,0:T(8,128)} %bitcast.1051), kind=kLoop, calls=%fused_computation.619 | loop fusion | bytes 2490368 | tf_op jit(solution)/shard_map/slice | solution.py:35
  168.7 2.3 fusion.90
  171.3 4.4 %constant_dynamic-update-slice_fusion.71 = (f32[8,72,2048]{2,0,1:T(8,128)S(1)}, f32[8,2048]{1,0:T(8,128)S(1)}, f32[8,2048]{1,0:T(8,128)S(1)}, f32[8,2048]{1,0:T(...) fusion(f32[2048]{0:T(1024)} %bitcast.1349, ...), kind=kLoop, calls=%fused_computation.124 | loop fusion | flops 4931583 | bytes 9707520
  177.2 4.9 %copy.427 = f32[8,72,2048]{2,1,0:T(8,128)} copy(f32[8,72,2048]{2,0,1:T(8,128)S(1)} %constant_dynamic-update-slice_fusion) | data formatting | bytes 9437184 | tf_op jit(solution)/shard_map/stack | solution.py:49
  182.1 5.8 %copy.428 = f32[576,2048]{0,1:T(8,128)} copy(f32[576,2048]{1,0:T(8,128)} %bitcast.1052) | data formatting | bytes 9437184 | tf_op jit(solution)/shard_map/stack | solution.py:49
  187.9 7.0 %sub.2234 = f32[576,2048]{0,1:T(8,128)} subtract(f32[576,2048]{0,1:T(8,128)} %copy.428, f32[576,2048]{0,1:T(8,128)} %scatter_custom_fusion.3) | non-fusion elementwise | flops 1179648 | bytes 14155776 | tf_op jit(solution)/shard_map/sub | solution.py:49
  194.8 5.5 %gather_fusion = f32[768,576]{1,0:T(8,128)S(1)} fusion(f32[576,2048]{0,1:T(8,128)} %sub.2234, s32[1024]{0:T(1024)S(1)} %pad_clamp_fusion), kind=kCustom, calls=%fused_computation | custom fusion | bytes 3542016 | tf_op jit(solution)/shard_map/jit(_take)/gather | solution.py:124
  200.4 1.6 reshape.262
  202.0 5.9 %all-to-all-start.2 = ((f32[576,128,6]{0,2,1:T(8,128)}), f32[576,128,6]{0,2,1:T(8,128)}, u32[]{:S(2)}, u32[]{:S(2)}) async-start(f32[576,128,6]{0,2,1:T(8,128)} %reshape.262), calls=%async_computation.2 | async-start | bytes 5242880 | tf_op jit(solution)/shard_map/all_to_all | solution.py:61
  207.9 12.5 %gather_fusion.2 = f32[2048,576]{1,0:T(8,128)} fusion(f32[576,2048]{0,1:T(8,128)} %sub.2234, s32[2048]{0:T(1024)S(1)} %copy-done.68), kind=kCustom, calls=%fused_computation.2 | custom fusion | bytes 9445376 | tf_op jit(solution)/shard_map/jit(_take)/gather | solution.py:129
  220.4 5.7 %copy.430 = f32[576,2048]{1,0:T(8,128)} copy(f32[576,2048]{0,1:T(8,128)} %bitcast.1043) | data formatting | bytes 9437184 | tf_op jit(solution)/shard_map/jit(_take)/gather | solution.py:129
  226.1 5.6 %copy.513 = f32[72,8,16,128]{3,2,1,0:T(8,128)} copy(f32[72,8,16,128]{3,1,2,0:T(8,128)} %bitcast.1053) | data formatting | bytes 9437184
  231.7 11.2 %all-to-all-done.2 = f32[576,128,6]{0,2,1:T(8,128)} async-done(((f32[576,128,6]{0,2,1:T(8,128)}), f32[576,128,6]{0,2,1:T(8,128)}, u32[]{:S(2)}, u32[]{:S(2)}) %all-to-all-start.2) | async-done | bytes 1769504 | tf_op jit(solution)/shard_map/all_to_all | solution.py:61
  242.9 2.4 reshape.263
  245.4 9.3 %gather_fusion.1 = f32[2048,576]{1,0:T(8,128)} fusion(f32[576,768]{0,1:T(8,128)S(1)} %reshape.263, s32[2048]{0:T(1024)S(1)} %copy-done.67), kind=kCustom, calls=%fused_computation.1 | custom fusion | bytes 9445376 | tf_op jit(solution)/shard_map/jit(_take)/gather | solution.py:126
  254.7 5.7 %copy.429 = f32[576,2048]{1,0:T(8,128)} copy(f32[576,2048]{0,1:T(8,128)} %bitcast.1044) | data formatting | bytes 9437184 | tf_op jit(solution)/shard_map/jit(_take)/gather | solution.py:126
  260.5 3.6 copy.512
  264.2 3.8 fusion.4
  268.5 1.3 collective-permute-start.1
  269.8 3.7 collective-permute-done.1
  273.5 2.8 collective-permute-done
  276.3 3.4 pad_maximum_fusion
  279.7 12.0 %fusion.241 = (f32[8,72,18,1]{3,2,1,0:T(8,128)}, f32[8,72,18,1]{3,2,1,0:T(8,128)}) fusion(f32[8,72,18,128]{3,2,1,0:T(8,128)} %pad_maximum_fusion), kind=kLoop, calls=%fused_computation.614 | loop fusion | bytes 165888 | tf_op jit(solution)/shard_map/slice | solution.py:12
  291.7 4.8 %copy.431 = f32[8,72,18,1]{1,0,3,2:T(8,128)S(1)} copy(f32[8,72,18,1]{3,2,1,0:T(8,128)} %get-tuple-element.226) | data formatting | bytes 82944 | tf_op jit(solution)/shard_map/slice | solution.py:12
  296.5 1.1 collective-permute-start.2
  297.7 4.8 %copy.433 = f32[8,72,18,1]{1,0,3,2:T(8,128)S(1)} copy(f32[8,72,18,1]{3,2,1,0:T(8,128)} %get-tuple-element.227) | data formatting | bytes 82944 | tf_op jit(solution)/shard_map/slice | solution.py:13
  303.0 4.8 %copy.432 = f32[8,72,18,1]{3,2,1,0:T(8,128)} copy(f32[8,72,18,1]{1,0,3,2:T(8,128)S(1)} %collective-permute-done.2) | data formatting | bytes 82944 | tf_op jit(solution)/shard_map/ppermute | solution.py:18
  307.8 1.3 collective-permute-done.3
  309.1 4.5 %copy.434 = f32[8,72,18,1]{3,2,1,0:T(8,128)} copy(f32[8,72,18,1]{1,0,3,2:T(8,128)S(1)} %collective-permute-done.3) | data formatting | bytes 82944 | tf_op jit(solution)/shard_map/ppermute | solution.py:16
  313.6 15.8 %fusion.12 = f32[8,72,16,128]{3,2,1,0:T(8,128)S(1)} fusion(f32[8,72,18,1]{3,2,1,0:T(8,128)} %copy.434, f32[8,72,1,128]{3,2,1,0:T(1,128)S(1)} %collective-permute-done, f32[8,72,16,128]{3,2,1,0:T(8,128)} %copy-done, f32[8,72,1,128]{3,2,1,0:T(1,128)S(1)} %collective-permute-done.1, f32[8,72,18,1]{3,2,1,0:T(8,128)} %copy.432), kind=kLoop, calls=%fused_computation.32 | loop fusion | flops 15335424 | bytes 10109952 | tf_op jit(solution)/shard_map/sub | solution.py:67
  329.9 1.6 collective-permute-start.5
  331.5 1.7 collective-permute-start.4
  333.2 2.0 collective-permute-done.5
  335.1 2.8 collective-permute-done.4
  337.9 3.4 pad_maximum_fusion.1
  341.3 12.0 %fusion.240 = (f32[8,72,18,1]{3,2,1,0:T(8,128)}, f32[8,72,18,1]{3,2,1,0:T(8,128)}) fusion(f32[8,72,18,128]{3,2,1,0:T(8,128)} %pad_maximum_fusion.1), kind=kLoop, calls=%fused_computation.613 | loop fusion | bytes 165888 | tf_op jit(solution)/shard_map/slice | solution.py:12
  353.4 4.8 %copy.435 = f32[8,72,18,1]{1,0,3,2:T(8,128)S(1)} copy(f32[8,72,18,1]{3,2,1,0:T(8,128)} %get-tuple-element.224) | data formatting | bytes 82944 | tf_op jit(solution)/shard_map/slice | solution.py:12
  358.2 1.9 collective-permute-start.6
  360.1 4.8 %copy.437 = f32[8,72,18,1]{1,0,3,2:T(8,128)S(1)} copy(f32[8,72,18,1]{3,2,1,0:T(8,128)} %get-tuple-element.225) | data formatting | bytes 82944 | tf_op jit(solution)/shard_map/slice | solution.py:13
  365.0 4.9 %copy.436 = f32[8,72,18,1]{3,2,1,0:T(8,128)} copy(f32[8,72,18,1]{1,0,3,2:T(8,128)S(1)} %collective-permute-done.6) | data formatting | bytes 82944 | tf_op jit(solution)/shard_map/ppermute | solution.py:18
  369.9 1.6 collective-permute-done.7
  371.5 4.5 %copy.438 = f32[8,72,18,1]{3,2,1,0:T(8,128)} copy(f32[8,72,18,1]{1,0,3,2:T(8,128)S(1)} %collective-permute-done.7) | data formatting | bytes 82944 | tf_op jit(solution)/shard_map/ppermute | solution.py:16
  376.0 18.3 %fusion.8 = f32[8,72,16,128]{3,2,1,0:T(8,128)} fusion(f32[8,72,16,128]{3,2,1,0:T(8,128)} %copy-done, f32[8,72,18,1]{3,2,1,0:T(8,128)} %copy.438, f32[8,72,1,128]{3,2,1,0:T(1,128)S(1)} %collective-permute-done.4, f32[8,72,16,128]{3,2,1,0:T(8,128)} %copy-done.1, f32[8,72,1,128]{3,2,1,0:T(1,128)S(1)} %collective-permute-done.5, f32[8,72,18,1]{3,2,1,0:T(8,128)} %copy.436), kind=kLoop, calls=%fused_computation.20 | loop fusion | flops 17694720 | bytes 14828544 | tf_op jit(solution)/shard_map/sub | solution.py:133
  (240 shorter events, 8.3 us)
Async XLA Ops:
  1.5 37.8 %copy-start.69 = (pred[16,128]{1,0:T(8,128)(4,1)}, pred[16,128]{1,0:T(8,128)(4,1)S(1)}, u32[]{:S(2)}) copy-start(pred[16,128]{1,0:T(8,128)(4,1)S(1)} %get-tuple-element.223) | copy-start | bytes 6148
  16.1 64.7 %all-to-all-start = ((s32[1,128,6]{2,0,1:T(1,128)}), s32[1,128,6]{2,0,1:T(1,128)S(1)}, u32[]{:S(2)}, u32[]{:S(2)}) async-start(s32[1,128,6]{2,0,1:T(1,128)} %bitcast.7), calls=%async_computation | async-start | bytes 131072 | tf_op jit(solution)/shard_map/all_to_all | solution.py:55
  79.2 11.4 %copy-start.3 = (f32[72,2048]{1,0:T(8,128)S(1)}, f32[72,2048]{1,0:T(8,128)}, u32[]{:S(2)}) copy-start(f32[72,2048]{1,0:T(8,128)} %param.8) | copy-start | bytes 1769476
  80.8 45.2 %all-to-all-start.1 = ((f32[576,128,6]{0,2,1:T(8,128)}), f32[576,128,6]{0,2,1:T(8,128)S(1)}, u32[]{:S(2)}, u32[]{:S(2)}) async-start(f32[576,128,6]{0,2,1:T(8,128)} %reshape.259), calls=%async_computation.1 | async-start | bytes 5242880 | tf_op jit(solution)/shard_map/all_to_all | solution.py:54
  144.1 24.3 %copy-start.5 = (f32[1,2048]{1,0:T(1,128)S(1)}, f32[1,2048]{1,0:T(1,128)}, u32[]{:S(2)}) copy-start(f32[1,2048]{1,0:T(1,128)} %copy-done.4) | copy-start | bytes 24580
  144.1 24.4 %copy-start.7 = (f32[1,2048]{1,0:T(1,128)S(1)}, f32[1,2048]{1,0:T(1,128)}, u32[]{:S(2)}) copy-start(f32[1,2048]{1,0:T(1,128)} %copy-done.6) | copy-start | bytes 24580
  144.1 24.4 %copy-start.9 = (f32[1,2048]{1,0:T(1,128)S(1)}, f32[1,2048]{1,0:T(1,128)}, u32[]{:S(2)}) copy-start(f32[1,2048]{1,0:T(1,128)} %copy-done.8) | copy-start | bytes 24580
  144.1 24.4 %copy-start.11 = (f32[1,2048]{1,0:T(1,128)S(1)}, f32[1,2048]{1,0:T(1,128)}, u32[]{:S(2)}) copy-start(f32[1,2048]{1,0:T(1,128)} %copy-done.10) | copy-start | bytes 24580
  144.1 24.4 %copy-start.12 = (f32[1,2048]{1,0:T(1,128)S(1)}, f32[1,2048]{1,0:T(1,128)}, u32[]{:S(2)}) copy-start(f32[1,2048]{1,0:T(1,128)} %get-tuple-element.71) | copy-start | bytes 24580
  144.1 24.4 %copy-start.13 = (f32[1,2048]{1,0:T(1,128)S(1)}, f32[1,2048]{1,0:T(1,128)}, u32[]{:S(2)}) copy-start(f32[1,2048]{1,0:T(1,128)} %get-tuple-element.75) | copy-start | bytes 24580
  144.1 24.4 %copy-start.14 = (f32[1,2048]{1,0:T(1,128)S(1)}, f32[1,2048]{1,0:T(1,128)}, u32[]{:S(2)}) copy-start(f32[1,2048]{1,0:T(1,128)} %get-tuple-element.79) | copy-start | bytes 24580
  144.1 24.4 %copy-start.15 = (f32[1,2048]{1,0:T(1,128)S(1)}, f32[1,2048]{1,0:T(1,128)}, u32[]{:S(2)}) copy-start(f32[1,2048]{1,0:T(1,128)} %get-tuple-element.83) | copy-start | bytes 24580
  144.1 24.4 %copy-start.16 = (f32[1,2048]{1,0:T(1,128)S(1)}, f32[1,2048]{1,0:T(1,128)}, u32[]{:S(2)}) copy-start(f32[1,2048]{1,0:T(1,128)} %get-tuple-element.87) | copy-start | bytes 24580
  144.1 24.4 %copy-start.17 = (f32[1,2048]{1,0:T(1,128)S(1)}, f32[1,2048]{1,0:T(1,128)}, u32[]{:S(2)}) copy-start(f32[1,2048]{1,0:T(1,128)} %get-tuple-element.91) | copy-start | bytes 24580
  144.2 24.4 %copy-start.18 = (f32[1,2048]{1,0:T(1,128)S(1)}, f32[1,2048]{1,0:T(1,128)}, u32[]{:S(2)}) copy-start(f32[1,2048]{1,0:T(1,128)} %get-tuple-element.95) | copy-start | bytes 24580
  144.2 24.4 %copy-start.19 = (f32[1,2048]{1,0:T(1,128)S(1)}, f32[1,2048]{1,0:T(1,128)}, u32[]{:S(2)}) copy-start(f32[1,2048]{1,0:T(1,128)} %get-tuple-element.99) | copy-start | bytes 24580
  144.2 24.4 %copy-start.20 = (f32[1,2048]{1,0:T(1,128)S(1)}, f32[1,2048]{1,0:T(1,128)}, u32[]{:S(2)}) copy-start(f32[1,2048]{1,0:T(1,128)} %get-tuple-element.103) | copy-start | bytes 24580
  144.2 24.4 %copy-start.21 = (f32[1,2048]{1,0:T(1,128)S(1)}, f32[1,2048]{1,0:T(1,128)}, u32[]{:S(2)}) copy-start(f32[1,2048]{1,0:T(1,128)} %get-tuple-element.107) | copy-start | bytes 24580
  144.2 24.4 %copy-start.22 = (f32[1,2048]{1,0:T(1,128)S(1)}, f32[1,2048]{1,0:T(1,128)}, u32[]{:S(2)}) copy-start(f32[1,2048]{1,0:T(1,128)} %get-tuple-element.111) | copy-start | bytes 24580
  144.2 24.4 %copy-start.23 = (f32[1,2048]{1,0:T(1,128)S(1)}, f32[1,2048]{1,0:T(1,128)}, u32[]{:S(2)}) copy-start(f32[1,2048]{1,0:T(1,128)} %get-tuple-element.115) | copy-start | bytes 24580
  144.2 24.4 %copy-start.24 = (f32[1,2048]{1,0:T(1,128)S(1)}, f32[1,2048]{1,0:T(1,128)}, u32[]{:S(2)}) copy-start(f32[1,2048]{1,0:T(1,128)} %get-tuple-element.119) | copy-start | bytes 24580
  144.2 24.4 %copy-start.25 = (f32[1,2048]{1,0:T(1,128)S(1)}, f32[1,2048]{1,0:T(1,128)}, u32[]{:S(2)}) copy-start(f32[1,2048]{1,0:T(1,128)} %get-tuple-element.123) | copy-start | bytes 24580
  144.2 24.4 %copy-start.26 = (f32[1,2048]{1,0:T(1,128)S(1)}, f32[1,2048]{1,0:T(1,128)}, u32[]{:S(2)}) copy-start(f32[1,2048]{1,0:T(1,128)} %get-tuple-element.127) | copy-start | bytes 24580
  144.2 24.4 %copy-start.27 = (f32[1,2048]{1,0:T(1,128)S(1)}, f32[1,2048]{1,0:T(1,128)}, u32[]{:S(2)}) copy-start(f32[1,2048]{1,0:T(1,128)} %get-tuple-element.131) | copy-start | bytes 24580
  144.3 24.4 %copy-start.28 = (f32[1,2048]{1,0:T(1,128)S(1)}, f32[1,2048]{1,0:T(1,128)}, u32[]{:S(2)}) copy-start(f32[1,2048]{1,0:T(1,128)} %get-tuple-element.135) | copy-start | bytes 24580
  144.3 24.4 %copy-start.29 = (f32[1,2048]{1,0:T(1,128)S(1)}, f32[1,2048]{1,0:T(1,128)}, u32[]{:S(2)}) copy-start(f32[1,2048]{1,0:T(1,128)} %get-tuple-element.139) | copy-start | bytes 24580
  144.3 24.4 %copy-start.30 = (f32[1,2048]{1,0:T(1,128)S(1)}, f32[1,2048]{1,0:T(1,128)}, u32[]{:S(2)}) copy-start(f32[1,2048]{1,0:T(1,128)} %get-tuple-element.143) | copy-start | bytes 24580
  156.0 15.0 %copy-start.31 = (f32[2048]{0:T(1024)S(1)}, f32[2048]{0:T(1024)}, u32[]{:S(2)}) copy-start(f32[2048]{0:T(1024)} %get-tuple-element.147) | copy-start | bytes 24580
  156.0 15.0 %copy-start.32 = (f32[2048]{0:T(1024)S(1)}, f32[2048]{0:T(1024)}, u32[]{:S(2)}) copy-start(f32[2048]{0:T(1024)} %get-tuple-element.151) | copy-start | bytes 24580
  156.0 15.0 %copy-start.33 = (f32[2048]{0:T(1024)S(1)}, f32[2048]{0:T(1024)}, u32[]{:S(2)}) copy-start(f32[2048]{0:T(1024)} %get-tuple-element.155) | copy-start | bytes 24580
  156.0 15.0 %copy-start.34 = (f32[2048]{0:T(1024)S(1)}, f32[2048]{0:T(1024)}, u32[]{:S(2)}) copy-start(f32[2048]{0:T(1024)} %get-tuple-element.159) | copy-start | bytes 24580
  156.1 15.0 %copy-start.35 = (f32[2048]{0:T(1024)S(1)}, f32[2048]{0:T(1024)}, u32[]{:S(2)}) copy-start(f32[2048]{0:T(1024)} %get-tuple-element.163) | copy-start | bytes 24580
  156.1 15.0 %copy-start.36 = (f32[2048]{0:T(1024)S(1)}, f32[2048]{0:T(1024)}, u32[]{:S(2)}) copy-start(f32[2048]{0:T(1024)} %get-tuple-element.167) | copy-start | bytes 24580
  156.1 15.0 %copy-start.37 = (f32[2048]{0:T(1024)S(1)}, f32[2048]{0:T(1024)}, u32[]{:S(2)}) copy-start(f32[2048]{0:T(1024)} %get-tuple-element.171) | copy-start | bytes 24580
  156.1 15.0 %copy-start.38 = (f32[2048]{0:T(1024)S(1)}, f32[2048]{0:T(1024)}, u32[]{:S(2)}) copy-start(f32[2048]{0:T(1024)} %get-tuple-element.175) | copy-start | bytes 24580
  156.1 15.0 %copy-start.39 = (f32[2048]{0:T(1024)S(1)}, f32[2048]{0:T(1024)}, u32[]{:S(2)}) copy-start(f32[2048]{0:T(1024)} %get-tuple-element.179) | copy-start | bytes 24580
  156.1 15.0 %copy-start.40 = (f32[2048]{0:T(1024)S(1)}, f32[2048]{0:T(1024)}, u32[]{:S(2)}) copy-start(f32[2048]{0:T(1024)} %get-tuple-element.183) | copy-start | bytes 24580
  156.1 15.0 %copy-start.41 = (f32[2048]{0:T(1024)S(1)}, f32[2048]{0:T(1024)}, u32[]{:S(2)}) copy-start(f32[2048]{0:T(1024)} %get-tuple-element.187) | copy-start | bytes 24580
  156.1 15.0 %copy-start.42 = (f32[2048]{0:T(1024)S(1)}, f32[2048]{0:T(1024)}, u32[]{:S(2)}) copy-start(f32[2048]{0:T(1024)} %get-tuple-element.191) | copy-start | bytes 24580
  156.1 15.0 %copy-start.43 = (f32[2048]{0:T(1024)S(1)}, f32[2048]{0:T(1024)}, u32[]{:S(2)}) copy-start(f32[2048]{0:T(1024)} %get-tuple-element.195) | copy-start | bytes 24580
  156.1 15.0 %copy-start.44 = (f32[2048]{0:T(1024)S(1)}, f32[2048]{0:T(1024)}, u32[]{:S(2)}) copy-start(f32[2048]{0:T(1024)} %get-tuple-element.199) | copy-start | bytes 24580
  156.2 15.0 %copy-start.45 = (f32[1,2048]{1,0:T(1,128)S(1)}, f32[1,2048]{1,0:T(1,128)}, u32[]{:S(2)}) copy-start(f32[1,2048]{1,0:T(1,128)} %get-tuple-element.60) | copy-start | bytes 24580
  156.2 15.0 %copy-start.46 = (f32[1,2048]{1,0:T(1,128)S(1)}, f32[1,2048]{1,0:T(1,128)}, u32[]{:S(2)}) copy-start(f32[1,2048]{1,0:T(1,128)} %get-tuple-element.64) | copy-start | bytes 24580
  156.2 15.0 %copy-start.47 = (f32[1,2048]{1,0:T(1,128)S(1)}, f32[1,2048]{1,0:T(1,128)}, u32[]{:S(2)}) copy-start(f32[1,2048]{1,0:T(1,128)} %get-tuple-element.68) | copy-start | bytes 24580
  171.2 4.8 %copy-start.58 = (f32[1,2048]{1,0:T(1,128)S(1)}, f32[1,2048]{1,0:T(1,128)}, u32[]{:S(2)}) copy-start(f32[1,2048]{1,0:T(1,128)} %get-tuple-element.112) | copy-start | bytes 24580
  171.2 4.9 %copy-start.57 = (f32[1,2048]{1,0:T(1,128)S(1)}, f32[1,2048]{1,0:T(1,128)}, u32[]{:S(2)}) copy-start(f32[1,2048]{1,0:T(1,128)} %get-tuple-element.108) | copy-start | bytes 24580
  171.2 4.9 %copy-start.56 = (f32[1,2048]{1,0:T(1,128)S(1)}, f32[1,2048]{1,0:T(1,128)}, u32[]{:S(2)}) copy-start(f32[1,2048]{1,0:T(1,128)} %get-tuple-element.104) | copy-start | bytes 24580
  171.2 5.0 %copy-start.55 = (f32[1,2048]{1,0:T(1,128)S(1)}, f32[1,2048]{1,0:T(1,128)}, u32[]{:S(2)}) copy-start(f32[1,2048]{1,0:T(1,128)} %get-tuple-element.100) | copy-start | bytes 24580
  171.2 5.0 %copy-start.54 = (f32[1,2048]{1,0:T(1,128)S(1)}, f32[1,2048]{1,0:T(1,128)}, u32[]{:S(2)}) copy-start(f32[1,2048]{1,0:T(1,128)} %get-tuple-element.96) | copy-start | bytes 24580
  171.3 5.0 %copy-start.53 = (f32[1,2048]{1,0:T(1,128)S(1)}, f32[1,2048]{1,0:T(1,128)}, u32[]{:S(2)}) copy-start(f32[1,2048]{1,0:T(1,128)} %get-tuple-element.92) | copy-start | bytes 24580
  171.3 5.1 %copy-start.52 = (f32[1,2048]{1,0:T(1,128)S(1)}, f32[1,2048]{1,0:T(1,128)}, u32[]{:S(2)}) copy-start(f32[1,2048]{1,0:T(1,128)} %get-tuple-element.88) | copy-start | bytes 24580
  200.4 7.5 %copy-start.68 = (s32[2048]{0:T(1024)S(1)}, s32[2048]{0:T(1024)}, u32[]{:S(2)}) copy-start(s32[2048]{0:T(1024)} %get-tuple-element.377) | copy-start | bytes 24580
  202.0 41.0 %all-to-all-start.2 = ((f32[576,128,6]{0,2,1:T(8,128)}), f32[576,128,6]{0,2,1:T(8,128)}, u32[]{:S(2)}, u32[]{:S(2)}) async-start(f32[576,128,6]{0,2,1:T(8,128)} %reshape.262), calls=%async_computation.2 | async-start | bytes 5242880 | tf_op jit(solution)/shard_map/all_to_all | solution.py:61
  226.1 19.3 %copy-start.67 = (s32[2048]{0:T(1024)S(1)}, s32[2048]{0:T(1024)}, u32[]{:S(2)}) copy-start(s32[2048]{0:T(1024)} %get-tuple-element.5) | copy-start | bytes 24580
  268.1 8.2 %copy-start = (f32[8,72,16,128]{3,2,1,0:T(8,128)}, f32[8,72,16,128]{3,2,1,0:T(8,128)S(1)}, u32[]{:S(2)}) copy-start(f32[8,72,16,128]{3,2,1,0:T(8,128)S(1)} %fusion.4) | copy-start | bytes 14155780
  268.5 5.0 %collective-permute-start.1 = (f32[8,72,1,128]{3,2,1,0:T(1,128)S(1)}, f32[8,72,1,128]{3,2,1,0:T(1,128)S(1)}, u32[]{:S(2)}, u32[]{:S(2)}) collective-permute-start(f32[8,72,1,128]{3,2,1,0:T(1,128)S(1)} %get-tuple-element.230), channel_id=1, source_target_pairs={{0,16},{16,32},{32,48},{48,64},{64,80},{80,96},{96,112},{112,0},{1... | collective-permute-start | bytes 884744 | tf_op jit(solution)/shard_map/ppermute | solution.py:16
  269.8 6.4 %collective-permute-start = (f32[8,72,1,128]{3,2,1,0:T(1,128)S(1)}, f32[8,72,1,128]{3,2,1,0:T(1,128)S(1)}, u32[]{:S(2)}, u32[]{:S(2)}) collective-permute-start(f32[8,72,1,128]{3,2,1,0:T(1,128)S(1)} %get-tuple-element.231), channel_id=1, source_target_pairs={{16,0},{32,16},{48,32},{64,48},{80,64},{96,80},{112,96},{0,112},{1... | collective-permute-start | bytes 884744 | tf_op jit(solution)/shard_map/ppermute | solution.py:18
  296.5 6.5 %collective-permute-start.2 = (f32[8,72,18,1]{1,0,3,2:T(8,128)S(1)}, f32[8,72,18,1]{1,0,3,2:T(8,128)S(1)}, u32[]{:S(2)}, u32[]{:S(2)}) collective-permute-start(f32[8,72,18,1]{1,0,3,2:T(8,128)S(1)} %copy.431), channel_id=1, source_target_pairs={{1,0},{2,1},{3,2},{4,3},{5,4},{6,5},{7,6},{8,7},{9,8},{10,9},{11,1... | collective-permute-start | bytes 124424 | tf_op jit(solution)/shard_map/ppermute | solution.py:18
  302.5 6.6 %collective-permute-start.3 = (f32[8,72,18,1]{1,0,3,2:T(8,128)S(1)}, f32[8,72,18,1]{1,0,3,2:T(8,128)S(1)}, u32[]{:S(2)}, u32[]{:S(2)}) collective-permute-start(f32[8,72,18,1]{1,0,3,2:T(8,128)S(1)} %copy.433), channel_id=1, source_target_pairs={{0,1},{1,2},{2,3},{3,4},{4,5},{5,6},{6,7},{7,8},{8,9},{9,10},{10,1... | collective-permute-start | bytes 124424 | tf_op jit(solution)/shard_map/ppermute | solution.py:16
  329.4 8.5 %copy-start.1 = (f32[8,72,16,128]{3,2,1,0:T(8,128)}, f32[8,72,16,128]{3,2,1,0:T(8,128)S(1)}, u32[]{:S(2)}) copy-start(f32[8,72,16,128]{3,2,1,0:T(8,128)S(1)} %fusion.12) | copy-start | bytes 14155780
  329.9 5.3 %collective-permute-start.5 = (f32[8,72,1,128]{3,2,1,0:T(1,128)S(1)}, f32[8,72,1,128]{3,2,1,0:T(1,128)S(1)}, u32[]{:S(2)}, u32[]{:S(2)}) collective-permute-start(f32[8,72,1,128]{3,2,1,0:T(1,128)S(1)} %get-tuple-element.228), channel_id=1, source_target_pairs={{0,16},{16,32},{32,48},{48,64},{64,80},{80,96},{96,112},{112,0},{1... | collective-permute-start | bytes 884744 | tf_op jit(solution)/shard_map/ppermute | solution.py:16
  331.5 6.4 %collective-permute-start.4 = (f32[8,72,1,128]{3,2,1,0:T(1,128)S(1)}, f32[8,72,1,128]{3,2,1,0:T(1,128)S(1)}, u32[]{:S(2)}, u32[]{:S(2)}) collective-permute-start(f32[8,72,1,128]{3,2,1,0:T(1,128)S(1)} %get-tuple-element.229), channel_id=1, source_target_pairs={{16,0},{32,16},{48,32},{64,48},{80,64},{96,80},{112,96},{0,112},{1... | collective-permute-start | bytes 884744 | tf_op jit(solution)/shard_map/ppermute | solution.py:18
  358.2 6.8 %collective-permute-start.6 = (f32[8,72,18,1]{1,0,3,2:T(8,128)S(1)}, f32[8,72,18,1]{1,0,3,2:T(8,128)S(1)}, u32[]{:S(2)}, u32[]{:S(2)}) collective-permute-start(f32[8,72,18,1]{1,0,3,2:T(8,128)S(1)} %copy.435), channel_id=1, source_target_pairs={{1,0},{2,1},{3,2},{4,3},{5,4},{6,5},{7,6},{8,7},{9,8},{10,9},{11,1... | collective-permute-start | bytes 124424 | tf_op jit(solution)/shard_map/ppermute | solution.py:18
  364.9 6.6 %collective-permute-start.7 = (f32[8,72,18,1]{1,0,3,2:T(8,128)S(1)}, f32[8,72,18,1]{1,0,3,2:T(8,128)S(1)}, u32[]{:S(2)}, u32[]{:S(2)}) collective-permute-start(f32[8,72,18,1]{1,0,3,2:T(8,128)S(1)} %copy.437), channel_id=1, source_target_pairs={{0,1},{1,2},{2,3},{3,4},{4,5},{5,6},{6,7},{7,8},{8,9},{9,10},{10,1... | collective-permute-start | bytes 124424 | tf_op jit(solution)/shard_map/ppermute | solution.py:16
  (18 other events, 46.4 us)
where the time goes:
time: 402 us; the launch traced here: 395 us
  local copies, waits for them, and re-layouts  231 us (57%)
  other arithmetic  72.6 us (18%)
  waiting for transfers between devices  53.8 us (13%)
  starting transfers between devices  35.3 us (9%)
    slice x4, local copies, waits for them, and re-layouts, with_halo(): head = lax.slice_in_dim(cells, 0, width, axis=dim)  33.7 us
    all_to_all x1, waiting for transfers between devices, trade_pair(): lax.all_to_all(values, ('fx', 'fy'), split_axis=1, concat_axis=1, tiled=T...  28.5 us
    slice x4, local copies, waits for them, and re-layouts, column_solve(): right_side = columns[:, level]  23.9 us
    scatter x1, local copies, waits for them, and re-layouts, local(): group_state = jnp.zeros((column_width, columns_dev), jnp.float32).at[:, k...  23.5 us
    sub x1, other arithmetic, local(): return updated - hyper_rate * smoothed  18.3 us
    gather x2, local copies, waits for them, and re-layouts, local(): kept_change = jnp.take(group_change, slot_index, axis=1, mode='clip')  18.2 us
    unnamed x181, local copies, waits for them, and re-layouts  18 us
    scatter x2, local copies, waits for them, and re-layouts, local(): group_state.at[:, arrived_slots]  16.7 us
  transfers between devices with their start and end apart: 11, of which 8 were waited for; matrix products, arithmetic and copies ran while one was open for 26% of the time, Pallas kernels for 0%

commit v1 on v0

v1 whole, which is shorter than its diff:
```python
import jax
import jax.numpy as jnp
from jax import lax
from jax.experimental import pallas as pl
from jax.experimental.pallas import tpu as pltpu
from jax.sharding import PartitionSpec as P

MESH = pl.DeviceIdType.MESH
F32 = jnp.float32
BF16 = jnp.bfloat16
CAP = 6
N_FX, N_FY, DEV = 8, 16, 128
TR, LEV, CX, CY = 8, 72, 16, 128
SLOTS = 2048
VALS = LEV + TR
STRIDE = 24
UROWS = TR * STRIDE + 8


def iota(shape, dim):
    return lax.broadcasted_iota(jnp.int32, shape, dim)


def split2(x):
    hi = x.astype(BF16)
    lo = (x - hi.astype(F32)).astype(BF16)
    return hi, lo


def split3(x):
    hi = x.astype(BF16)
    rest = x - hi.astype(F32)
    mid = rest.astype(BF16)
    lo = (rest - mid.astype(F32)).astype(BF16)
    return hi, mid, lo


def peer_at(step, fx, fy):
    z, core = fx // 2, fx % 2
    x, y = fy // 4, fy % 4
    dz = (2 + 3 * (step // 32)) % 4
    dx = (2 + 3 * ((step // 8) % 4)) % 4
    dy = (2 + 3 * ((step // 2) % 4)) % 4
    dc = (step + 1) % 2
    px = ((z + dz) % 4) * 2 + (core + dc) % 2
    py = ((x + dx) % 4) * 4 + (y + dy) % 4
    return px, py


SELF_STEP = 2 * 32 + 2 * 8 + 2 * 2 + 1


def each_peer(action, fx, fy):
    def one(step, carry):
        action(*peer_at(step, fx, fy))
        return carry

    lax.fori_loop(0, SELF_STEP, one, 0)
    lax.fori_loop(SELF_STEP + 1, DEV, one, 0)


def exchange_kernel(
    tracers, dest, slot, diff, flux,
    ue, us,
    tv, dest_v, slot_v, table, table_t, onehot, onehot_own, rank_v,
    req, req_in, rep, rep_in, dsplit, kv_own, kv, edge_kv, edge_kv_in, kv_halo,
    halo, edge, edge_in, edge_all, edge_kv_all, ratio_own, ratio_halo, ratio_side,
    load_sem, tv_sem, req_s, req_r, rep_s, rep_r, row_s, row_r, edge_s, edge_r,
    kvrow_s, kvrow_r, kvedge_s, kvedge_r,
):
    fx, fy = lax.axis_index("fx"), lax.axis_index("fy")
    me = fx * N_FY + fy
    up, down = (fx + N_FX - 1) % N_FX, (fx + 1) % N_FX
    left, right = (fy + N_FY - 1) % N_FY, (fy + 1) % N_FY

    loads = [
        pltpu.make_async_copy(dest, dest_v, load_sem.at[0]),
        pltpu.make_async_copy(slot, slot_v, load_sem.at[1]),
        pltpu.make_async_copy(diff, table.at[pl.ds(0, LEV)], load_sem.at[2]),
        pltpu.make_async_copy(flux, table.at[pl.ds(LEV, TR)], load_sem.at[3]),
    ]
    for load in loads:
        load.start()
    tv_load = pltpu.make_async_copy(tracers, tv, tv_sem)
    tv_load.start()

    barrier = pltpu.get_barrier_semaphore()

    def hello(px, py):
        pl.semaphore_signal(barrier, inc=1, device_id=(px, py), device_id_type=MESH)

    each_peer(hello, fx, fy)

    loads[0].wait()
    loads[1].wait()
    lane128 = iota((DEV, CY), 1)
    sub128 = iota((DEV, CY), 0)
    prefix = jnp.concatenate(
        [jnp.where(sub128 < lane128, 1.0, 0.0), jnp.ones((DEV, CY), F32)], 1
    ).astype(BF16)

    kk = iota((16, CY), 0)

    def route(i, carry):
        seen, asked = carry
        d = dest_v[pl.ds(i, 1), :]
        d = jnp.where(d == me, -1, d)
        code = slot_v[pl.ds(i, 1), :] + 1
        match = jnp.where(d == sub128, 1.0, 0.0)
        mb = match.astype(BF16)
        counts = jnp.dot(mb, prefix, preferred_element_type=F32)
        rank = jnp.sum(match * (counts[:, :CY] + seen), axis=0, keepdims=True)
        rank_v[pl.ds(i, 1), :] = rank
        value = jnp.where(kk < 8, code >> 7, code & 127).astype(F32)
        pick = jnp.where((kk & 7).astype(F32) == rank, value, 0.0).astype(BF16)
        asked = asked + lax.dot_general(
            mb, pick, (((1,), (1,)), ((), ())), preferred_element_type=F32
        )
        return seen + counts[:, CY:], asked

    _, asked = lax.fori_loop(
        0, CX, route, (jnp.zeros((DEV, CY), F32), jnp.zeros((DEV, 16), F32))
    )
    codes = asked[:, 0:8] * 128.0 + asked[:, 8:16]
    req[:, 0, :] = jnp.concatenate([codes, jnp.zeros((DEV, CY - 8), F32)], 1)

    pl.semaphore_wait(barrier, DEV - 1)

    def ask(px, py):
        pltpu.make_async_remote_copy(
            req.at[px * N_FY + py], req_in.at[me], req_s, req_r,
            device_id=(px, py), device_id_type=MESH,
        ).start()

    each_peer(ask, fx, fy)
    req_in[me] = jnp.zeros((1, CY), F32)

    rows = []
    for t in range(TR):
        rows.append(
            pltpu.make_async_remote_copy(
                tracers.at[t, :, pl.ds(14, 2), :],
                halo.at[:, pl.ds(8 * t + 6, 2), :],
                row_s.at[t], row_r.at[t], device_id=(down, fy), device_id_type=MESH,
            )
        )
        rows.append(
            pltpu.make_async_remote_copy(
                tracers.at[t, :, pl.ds(0, 2), :],
                halo.at[:, pl.ds(8 * t + 8, 2), :],
                row_s.at[TR + t], row_r.at[TR + t], device_id=(up, fy), device_id_type=MESH,
            )
        )
    for copy in rows:
        copy.start()

    loads[2].wait()
    loads[3].wait()

    def flip(b, carry):
        cols = pl.ds(pl.multiple_of(b * 128, 128), 128)
        part = jnp.concatenate([table[:, cols], jnp.zeros((128 - VALS, 128), F32)], 0)
        hi, lo = split2(part.T)
        table_t[cols, pl.ds(0, 128)] = hi
        table_t[cols, pl.ds(128, 128)] = lo
        return carry

    lax.fori_loop(0, SLOTS // 128, flip, 0)

    pltpu.make_async_copy(req_in.at[pl.ds(0, DEV - 1)], req_in.at[pl.ds(0, DEV - 1)], req_r).wait()
    wanted = req_in[:, 0, :]
    slot_lane = (iota((DEV, SLOTS), 1) + 1).astype(F32)
    got = []
    for k in range(CAP):
        pick = jnp.where(wanted[:, k : k + 1] == slot_lane, 1.0, 0.0).astype(BF16)
        both = jnp.dot(pick, table_t[...], preferred_element_type=F32)
        got.append(both[:, :128] + both[:, 128:])
    for j in range(3):
        rep[:, j, :] = jnp.where(lane128 < 64, got[2 * j], pltpu.roll(got[2 * j + 1], 64, 1))
    tail = jnp.zeros((DEV, CY), F32)
    for k in range(CAP):
        shift = (16 * k - 64) % 128
        moved = pltpu.roll(got[k], shift, 1) if shift else got[k]
        tail = jnp.where(lane128 // 16 == k, moved, tail)
    rep[:, 3, :] = tail

    def answer(px, py):
        pltpu.make_async_remote_copy(
            rep.at[px * N_FY + py], rep_in.at[me], rep_s, rep_r,
            device_id=(px, py), device_id_type=MESH,
        ).start()

    each_peer(answer, fx, fy)
    rep_in[me] = jnp.zeros((4, CY), F32)

    tv_load.wait()
    lane16 = iota((CX, CY), 1)

    def pack(q, carry):
        acc = jnp.zeros((CX, CY), F32)
        for lg in range(4):
            for t in range(TR):
                cells = tv[t, q + 18 * lg]
                at = 32 * lg + 4 * t
                first = pltpu.roll(cells, at, 1) if at else cells
                last = pltpu.roll(cells, (at + 4) % 128, 1) if (at + 4) % 128 else cells
                acc = jnp.where((lane16 == at) | (lane16 == at + 1), first, acc)
                acc = jnp.where((lane16 == at + 2) | (lane16 == at + 3), last, acc)
        edge[q] = acc
        return carry

    lax.fori_loop(0, 18, pack, 0)

    def to_sides(source, target, sends, receives):
        places = [
            (fx, right, 0, 0, 16), (fx, left, 1, 0, 16),
            (down, right, 2, 8, 8), (down, left, 3, 8, 8),
            (up, right, 4, 0, 8), (up, left, 5, 0, 8),
        ]
        copies = [
            pltpu.make_async_remote_copy(
                source.at[:, pl.ds(first, count), :],
                target.at[n, :, pl.ds(first, count), :],
                sends.at[n], receives.at[n], device_id=(px, py), device_id_type=MESH,
            )
            for px, py, n, first, count in places
        ]
        for copy in copies:
            copy.start()
        return copies

    edges = to_sides(edge, edge_in, edge_s, edge_r)

    def spread(i, carry):
        cols = pl.ds(pl.multiple_of(i * CY, CY), CY)
        d = dest_v[pl.ds(i, 1), :]
        d = jnp.where(d == me, -1, d)
        rank = rank_v[pl.ds(i, 1), :]
        hit = d == sub128
        for k in range(CAP):
            onehot[pl.ds(k * DEV, DEV), cols] = jnp.where(
                hit & (rank == float(k)), 1.0, 0.0
            ).astype(BF16)
        return carry

    lax.fori_loop(0, CX, spread, 0)
    slot_sub = iota((SLOTS, CY), 0)
    tab3 = jnp.concatenate(split3(table[...]), 0)

    def keep(i, carry):
        for half in range(2):
            d = dest_v[pl.ds(2 * i + half, 1), :]
            s = jnp.where(d == me, slot_v[pl.ds(2 * i + half, 1), :], -1)
            onehot_own[:, pl.ds(half * CY, CY)] = jnp.where(s == slot_sub, 1.0, 0.0).astype(BF16)
        three = jnp.dot(tab3, onehot_own[...], preferred_element_type=F32)
        kv_own[:, pl.ds(pl.multiple_of(i * 2 * CY, 2 * CY), 2 * CY)] = (
            three[:VALS] + three[VALS : 2 * VALS] + three[2 * VALS :]
        )
        return carry

    lax.fori_loop(0, CX // 2, keep, 0)

    pltpu.make_async_copy(rep_in.at[pl.ds(0, DEV - 1)], rep_in.at[pl.ds(0, DEV - 1)], rep_r).wait()
    last = rep_in[:, 3, :]
    for k in range(CAP):
        main = rep_in[:, k // 2, :]
        if k % 2:
            main = pltpu.roll(main, 64, 1)
        shift = (64 - 16 * k) % 128
        end = pltpu.roll(last, shift, 1) if shift else last
        cols = jnp.where(lane128 < 64, main, jnp.where(lane128 < VALS, end, 0.0))
        hi, lo = split2(cols.T[:VALS])
        dsplit[pl.ds(0, VALS), pl.ds(k * DEV, DEV)] = hi
        dsplit[pl.ds(VALS, VALS), pl.ds(k * DEV, DEV)] = lo

    def assemble(i, carry):
        cols = pl.ds(pl.multiple_of(i * 2 * CY, 2 * CY), 2 * CY)
        two = jnp.dot(dsplit[...], onehot[:, cols], preferred_element_type=F32)
        full = kv_own[:, cols] + two[:VALS] + two[VALS:]
        kv[:, 2 * i, :] = full[:, :CY]
        kv[:, 2 * i + 1, :] = full[:, CY:]
        return carry

    for i in range(CX // 2):
        assemble(i, 0)

    kvrows = [
        pltpu.make_async_remote_copy(
            kv.at[:, pl.ds(14, 2), :], kv_halo.at[:, pl.ds(6, 2), :],
            kvrow_s.at[0], kvrow_r.at[0], device_id=(down, fy), device_id_type=MESH,
        ),
        pltpu.make_async_remote_copy(
            kv.at[:, pl.ds(0, 2), :], kv_halo.at[:, pl.ds(0, 2), :],
            kvrow_s.at[1], kvrow_r.at[1], device_id=(up, fy), device_id_type=MESH,
        ),
    ]
    for copy in kvrows:
        copy.start()
    for g in range(3):
        acc = jnp.zeros((CX, CY), F32)
        for m in range(32 if g < 2 else VALS - 64):
            moved = pltpu.roll(kv[32 * g + m], 4 * m + 2, 1) if 4 * m + 2 < 128 else kv[32 * g + m]
            acc = jnp.where(lane16 // 4 == m, moved, acc)
        edge_kv[g] = acc
    kvedges = to_sides(edge_kv, edge_kv_in, kvedge_s, kvedge_r)

    def factors(level, above_kv, here_kv, ratio):
        inner = (level < LEV - 1).astype(F32)
        above = above_kv * (level > 0).astype(F32)
        below = here_kv * inner
        pivot = 1.0 + above + here_kv - above * ratio
        inverse = 1.0 / pivot
        return below * inverse, inverse, above

    def forward(level, carry):
        ratio, partial = carry
        ratio, inverse, above = factors(level, kv[jnp.maximum(level - 1, 0)], kv[level], ratio)
        ratio_own[level] = ratio
        bottom = (level == LEV - 1).astype(F32)
        new = []
        for t in range(TR):
            g = (tv[t, level] + kv[LEV + t] * bottom + above * partial[t]) * inverse
            ue[level, pl.ds(STRIDE * t + 8, CX), :] = g
            new.append(g)
        return ratio, tuple(new)

    zero16 = jnp.zeros((CX, CY), F32)
    lax.fori_loop(0, LEV, forward, (zero16, (zero16,) * TR))

    def backward(step, below):
        level = LEV - 1 - step
        ratio = ratio_own[level]
        new = []
        for t in range(TR):
            rows_t = pl.ds(STRIDE * t + 8, CX)
            x = ue[level, rows_t, :] + ratio * below[t]
            ue[level, rows_t, :] = x
            new.append(x)
        return tuple(new)

    lax.fori_loop(0, LEV, backward, (zero16,) * TR)

    for copy in rows + edges:
        copy.wait_recv()
    lane8 = iota((8, CY), 1)
    sub8 = iota((8, CY), 0)

    def gather_edges(q, carry):
        edge_all[q, pl.ds(0, CX), :] = jnp.where(lane16 % 4 < 2, edge_in[1, q], edge_in[0, q])
        above = jnp.where(lane8 % 4 < 2, edge_in[3, q, pl.ds(8, 8)], edge_in[2, q, pl.ds(8, 8)])
        below = jnp.where(lane8 % 4 < 2, edge_in[5, q, pl.ds(0, 8)], edge_in[4, q, pl.ds(0, 8)])
        edge_all[q, pl.ds(CX, 8), :] = jnp.where(sub8 == 7, above, below)
        return carry

    lax.fori_loop(0, 18, gather_edges, 0)
    for copy in kvrows + kvedges:
        copy.wait_recv()
    for g in range(3):
        edge_kv_all[g, pl.ds(0, CX), :] = jnp.where(lane16 % 4 < 2, edge_kv_in[0, g], edge_kv_in[1, g])
        above = jnp.where(lane8 % 4 < 2, edge_kv_in[2, g, pl.ds(8, 8)], edge_kv_in[3, g, pl.ds(8, 8)])
        below = jnp.where(lane8 % 4 < 2, edge_kv_in[4, g, pl.ds(0, 8)], edge_kv_in[5, g, pl.ds(0, 8)])
        edge_kv_all[g, pl.ds(CX, 8), :] = jnp.where(sub8 == 7, above, below)

    lane24 = iota((24, CY), 1)
    quad = (lane24 + 2) % 4

    def side_kv(level):
        source = edge_kv_all[level // 32]
        return jnp.take_along_axis(source, 4 * (level % 32) + quad, axis=1)

    side_flux = jnp.take_along_axis(
        edge_kv_all[2], 32 + 4 * ((lane24 // 4) % 8) + quad, axis=1
    )

    def forward_rim(level, carry):
        ratio, partial, sratio, spartial, kv_above = carry
        bottom = (level == LEV - 1).astype(F32)
        ratio, inverse, above = factors(
            level, kv_halo[jnp.maximum(level - 1, 0)], kv_halo[level], ratio
        )
        ratio_halo[level] = ratio
        new = []
        for j in range(TR + 1):
            source = jnp.where(
                sub8 < 4, kv_halo[LEV + max(j - 1, 0)], kv_halo[LEV + min(j, TR - 1)]
            )
            g = (halo[level, pl.ds(8 * j, 8), :] + source * bottom + above * partial[j]) * inverse
            ue[level, pl.ds(STRIDE * j, 8), :] = g
            new.append(g)
        kv_here = side_kv(level)
        sratio, inverse, above = factors(level, kv_above, kv_here, sratio)
        ratio_side[level] = sratio
        raw = pltpu.roll(edge_all[level % 18], (128 - 32 * (level // 18)) % 128, 1)
        g = (raw + side_flux * bottom + above * spartial) * inverse
        us[level, pl.ds(8, 24), :] = g
        return ratio, tuple(new), sratio, g, kv_here

    zero8 = jnp.zeros((8, CY), F32)
    zero24 = jnp.zeros((24, CY), F32)
    lax.fori_loop(0, LEV, forward_rim, (zero8, (zero8,) * (TR + 1), zero24, zero24, zero24))

    def backward_rim(step, carry):
        level = LEV - 1 - step
        below, sbelow = carry
        ratio = ratio_halo[level]
        new = []
        for j in range(TR + 1):
            rows_j = pl.ds(STRIDE * j, 8)
            x = ue[level, rows_j, :] + ratio * below[j]
            ue[level, rows_j, :] = x
            new.append(x)
        x = us[level, pl.ds(8, 24), :] + ratio_side[level] * sbelow
        us[level, pl.ds(8, 24), :] = x
        us[level, pl.ds(0, 8), :] = x[16:24]
        return tuple(new), x

    lax.fori_loop(0, LEV, backward_rim, ((zero8,) * (TR + 1), zero24))

    for copy in rows + edges + kvrows + kvedges:
        copy.wait_send()
    pltpu.make_async_copy(req.at[pl.ds(0, DEV - 1)], req.at[pl.ds(0, DEV - 1)], req_s).wait()
    pltpu.make_async_copy(rep.at[pl.ds(0, DEV - 1)], rep.at[pl.ds(0, DEV - 1)], rep_s).wait()


def smooth_kernel(ue, us, out):
    block = pl.program_id(0)
    count = out.shape[1]
    lane = iota((CX, CY), 1)
    place = lane % 4
    rim = (lane < 2) | (lane >= CY - 2)

    def one(n, carry):
        level = block * count + n
        u = us[level, pl.ds(8, CX), :]
        p = 0.2 * u - 0.05 * (us[level, pl.ds(7, CX), :] + us[level, pl.ds(9, CX), :])
        cross = jnp.where(
            place == 1, pltpu.roll(p, 1, 1), jnp.where(place == 2, pltpu.roll(p, CY - 1, 1), 0.0)
        )
        side = cross - 0.025 * u
        for t in range(TR):
            row = STRIDE * t + 8
            u = ue[level, pl.ds(row, CX), :]
            near = ue[level, pl.ds(row - 1, CX), :] + ue[level, pl.ds(row + 1, CX), :]
            far = ue[level, pl.ds(row - 2, CX), :] + ue[level, pl.ds(row + 2, CX), :]
            p = 0.2 * u - 0.05 * near
            s = -0.025 * u
            west = p + jnp.where(lane == 0, 0.0, pltpu.roll(s, 1, 1))
            east = p + jnp.where(lane == CY - 1, 0.0, pltpu.roll(s, CY - 1, 1))
            west = jnp.where(lane == 0, 0.0, pltpu.roll(west, 1, 1))
            east = jnp.where(lane == CY - 1, 0.0, pltpu.roll(east, CY - 1, 1))
            outer = jnp.where(rim, pltpu.roll(side, (CY - 2 - 4 * t) % CY, 1), 0.0)
            out[t, n] = 0.5 * u + 0.2 * near - 0.025 * far + (west + east) + outer
        return carry

    lax.fori_loop(0, count, one, 0)


def local(tracers, group_dest, group_slot, diffusivity, surface_flux):
    any_spec = pl.BlockSpec(memory_space=pl.ANY)
    dma = pltpu.SemaphoreType.DMA
    ue, us = pl.pallas_call(
        exchange_kernel,
        out_shape=(
            pltpu.VMEM((LEV, UROWS, CY), F32),
            pltpu.VMEM((LEV, 32, CY), F32),
        ),
        in_specs=[any_spec] * 5,
        out_specs=(pl.BlockSpec(memory_space=pltpu.VMEM), pl.BlockSpec(memory_space=pltpu.VMEM)),
        scratch_shapes=[
            pltpu.VMEM((TR, LEV, CX, CY), F32),
            pltpu.VMEM((CX, CY), jnp.int32),
            pltpu.VMEM((CX, CY), jnp.int32),
            pltpu.VMEM((VALS, SLOTS), F32),
            pltpu.VMEM((SLOTS, 256), BF16),
            pltpu.VMEM((CAP * DEV, SLOTS), BF16),
            pltpu.VMEM((SLOTS, 256), BF16),
            pltpu.VMEM((CX, CY), F32),
            pltpu.VMEM((DEV, 1, CY), F32),
            pltpu.VMEM((DEV, 1, CY), F32),
            pltpu.VMEM((DEV, 4, CY), F32),
            pltpu.VMEM((DEV, 4, CY), F32),
            pltpu.VMEM((2 * VALS, CAP * DEV), BF16),
            pltpu.VMEM((VALS, SLOTS), F32),
            pltpu.VMEM((VALS, CX, CY), F32),
            pltpu.VMEM((3, CX, CY), F32),
            pltpu.VMEM((6, 3, CX, CY), F32),
            pltpu.VMEM((VALS, 8, CY), F32),
            pltpu.VMEM((LEV, 8 * (TR + 1), CY), F32),
            pltpu.VMEM((18, CX, CY), F32),
            pltpu.VMEM((6, 18, CX, CY), F32),
            pltpu.VMEM((18, 24, CY), F32),
            pltpu.VMEM((3, 24, CY), F32),
            pltpu.VMEM((LEV, CX, CY), F32),
            pltpu.VMEM((LEV, 8, CY), F32),
            pltpu.VMEM((LEV, 24, CY), F32),
            dma((4,)), dma, dma, dma, dma, dma,
            dma((2 * TR,)), dma((2 * TR,)), dma((6,)), dma((6,)),
            dma((2,)), dma((2,)), dma((6,)), dma((6,)),
        ],
        compiler_params=pltpu.CompilerParams(
            collective_id=0, has_side_effects=True, vmem_limit_bytes=44 << 20
        ),
        name="exchange",
    )(tracers, group_dest, group_slot, diffusivity, surface_flux)
    count = 9
    whole = pl.BlockSpec(memory_space=pltpu.VMEM)
    return pl.pallas_call(
        smooth_kernel,
        grid=(LEV // count,),
        out_shape=jax.ShapeDtypeStruct(tracers.shape, F32),
        in_specs=[whole, whole],
        out_specs=pl.BlockSpec((TR, count, CX, CY), lambda b: (0, b, 0, 0)),
        compiler_params=pltpu.CompilerParams(vmem_limit_bytes=20 << 20),
        name="smooth",
    )(ue, us)


def solution(mesh):
    placed = (
        P(None, None, "fx", "fy"),
        P("fx", "fy"),
        P("fx", "fy"),
        P(None, ("fx", "fy")),
        P(None, ("fx", "fy")),
    )
    return jax.shard_map(
        local, mesh=mesh, in_specs=placed, out_specs=P(None, None, "fx", "fy"), check_vma=False
    )
```

time: 402 us -> 77.7 us (0.19); the launches traced: 395 us -> 77.5 us
  local copies, waits for them, and re-layouts: 231 us -> 3.3 us
  Pallas kernels: 0 us -> 74.2 us
  other arithmetic: 72.6 us -> 0 us
  waiting for transfers between devices: 53.8 us -> 0 us
  starting transfers between devices: 35.3 us -> 0 us
    pallas_call x0 -> x2, Pallas kernels: none -> 74.2 us  [the longest x1 59.1 us: local(): pl.pallas_call(exchange_kernel, out_shape=(pltpu.VMEM((LEV, UROWS, CY), F...]
    slice x15 -> x0, local copies, waits for them, and re-layouts: 71 us -> none  [the longest x4 33.7 us: with_halo(): head = lax.slice_in_dim(cells, 0, width, axis=dim)]
    scatter x5 -> x0, local copies, waits for them, and re-layouts: 59 us -> none  [the longest x1 23.5 us: local(): group_state = jnp.zeros((column_width, columns_dev), jnp.float32).at[:, k...]
    sub x3 -> x0, other arithmetic: 41 us -> none  [the longest x1 18.3 us: local(): return updated - hyper_rate * smoothed]
    all_to_all x3 -> x0, waiting for transfers between devices: 39.7 us -> none  [the longest x1 28.5 us: trade_pair(): lax.all_to_all(values, ('fx', 'fy'), split_axis=1, concat_axis=1, tiled=T...]
    gather x5 -> x0, local copies, waits for them, and re-layouts: 38.8 us -> none  [the longest x2 18.2 us: local(): kept_change = jnp.take(group_change, slot_index, axis=1, mode='clip')]
    all_to_all x3 -> x0, starting transfers between devices: 27.2 us -> none  [the longest x1 11.5 us: trade_pair(): lax.all_to_all(slots, ('fx', 'fy'), split_axis=1, concat_axis=1, tiled=True)]
    ppermute x4 -> x0, local copies, waits for them, and re-layouts: 18.8 us -> none  [the longest x2 9.76 us: with_halo(): lax.ppermute(head, axis, [((i + 1) % count, i) for i in range(count)])]
  transfers between devices with their start and end apart: 11 -> 0, of which waited for: 8 -> 0; matrix products, arithmetic and copies ran while one was open for 26% -> 0% of each run, Pallas kernels for 0% -> 0%
where the time goes in v1:
time: 77.7 us; the launch traced here: 77.5 us
  Pallas kernels  74.2 us (95%)
  local copies, waits for them, and re-layouts  3.3 us (4%)
    pallas_call x1, Pallas kernels, local(): pl.pallas_call(exchange_kernel, out_shape=(pltpu.VMEM((LEV, UROWS, CY), F...  59.1 us
    pallas_call x1, Pallas kernels, local(): pl.pallas_call(smooth_kernel, grid=(LEV // count,), out_shape=jax.ShapeDt...  15.1 us
    unnamed x8, local copies, waits for them, and re-layouts  3.3 us

profile of v1, /device:TPU:1, one launch (start us, length us, event | category | flops | bytes accessed | tf_op | source)
XLA Modules:
  0.0 77.5 jit_solution(16244857791214469234)
XLA Ops:
  0.0 0.0 copy-start
  0.0 1.1 %copy-done = f32[72,2048]{1,0:T(8,128)S(1)} copy-done((f32[72,2048]{1,0:T(8,128)S(1)}, f32[72,2048]{1,0:T(8,128)}, u32[]{:S(2)}) %copy-start) | copy-done | bytes 589848
  1.1 0.0 copy-start.1
  1.1 0.8 %copy-done.1 = f32[8,2048]{1,0:T(8,128)S(1)} copy-done((f32[8,2048]{1,0:T(8,128)S(1)}, f32[8,2048]{1,0:T(8,128)}, u32[]{:S(2)}) %copy-start.1) | copy-done | bytes 65560
  1.9 0.0 copy-start.2
  1.9 0.7 copy-done.2
  2.6 0.0 copy-start.3
  2.6 0.7 copy-done.3
  3.3 59.1 %exchange.1 = (f32[72,200,128]{2,1,0:T(8,128)S(1)}, f32[72,32,128]{2,1,0:T(8,128)S(1)}) custom-call(f32[8,72,16,128]{3,2,1,0:T(8,128)} %tracers.1, s32[16,128]{1,0:T(8,128)S(1)} %copy-done.2, s32[16,128]{1,0:T(8,128)S(1)} %copy-done.3, f32[72,2048]{1,0:T(8,128)S(1)} %copy-done, f32[8,2048]{1,0:T(8,128)S(1)} %copy-done.1), custom_call_target="tpu_custom_call" | custom-call | tf_op jit(solution)/shard_map/exchange/pallas_call | solution.py:461
  62.4 15.1 %smooth.1 = f32[8,72,16,128]{3,2,1,0:T(8,128)} custom-call(f32[72,200,128]{2,1,0:T(8,128)S(1)} %get-tuple-element.7.ue, f32[72,32,128]{2,1,0:T(8,128)S(1)} %get-tuple-element.8.us), custom_call_target="tpu_custom_call" | custom-call | tf_op jit(solution)/shard_map/smooth/pallas_call | solution.py:507
Async XLA Ops:
  0.0 1.1 %copy-start = (f32[72,2048]{1,0:T(8,128)S(1)}, f32[72,2048]{1,0:T(8,128)}, u32[]{:S(2)}) copy-start(f32[72,2048]{1,0:T(8,128)} %diff.1) | copy-start | bytes 1769476
  1.1 0.8 %copy-start.1 = (f32[8,2048]{1,0:T(8,128)S(1)}, f32[8,2048]{1,0:T(8,128)}, u32[]{:S(2)}) copy-start(f32[8,2048]{1,0:T(8,128)} %flux.1) | copy-start | bytes 196612
  1.9 0.7 copy-start.2
  2.6 0.7 copy-start.3

commit v2 on v1

v2 whole, which is shorter than its diff:
```python
import jax
import jax.numpy as jnp
from jax import lax
from jax.experimental import pallas as pl
from jax.experimental.pallas import tpu as pltpu
from jax.sharding import PartitionSpec as P

MESH = pl.DeviceIdType.MESH
F32 = jnp.float32
BF16 = jnp.bfloat16
CAP = 6
N_FX, N_FY, DEV = 8, 16, 128
TR, LEV, CX, CY = 8, 72, 16, 128
SLOTS = 2048
VALS = LEV + TR
STRIDE = 24
UROWS = TR * STRIDE + 8


def iota(shape, dim):
    return lax.broadcasted_iota(jnp.int32, shape, dim)


def split2(x):
    hi = x.astype(BF16)
    lo = (x - hi.astype(F32)).astype(BF16)
    return hi, lo


def split3(x):
    hi = x.astype(BF16)
    rest = x - hi.astype(F32)
    mid = rest.astype(BF16)
    lo = (rest - mid.astype(F32)).astype(BF16)
    return hi, mid, lo


HOPS = (0, 1, 2, 1)
STEPS = sorted(
    (
        (dz, dx, dy, dc)
        for dz in range(4) for dx in range(4) for dy in range(4) for dc in range(2)
        if dz or dx or dy or dc
    ),
    key=lambda d: -(HOPS[d[0]] + HOPS[d[1]] + HOPS[d[2]]),
)


def all_peers(fx, fy):
    z, core, x, y = fx // 2, fx % 2, fy // 4, fy % 4
    zs, cores = [(z + d) % 4 * 2 for d in range(4)], [core, 1 - core]
    xs, ys = [(x + d) % 4 * 4 for d in range(4)], [(y + d) % 4 for d in range(4)]
    on_fx = {(dz, dc): zs[dz] + cores[dc] for dz in range(4) for dc in range(2)}
    on_fy = {(dx, dy): xs[dx] + ys[dy] for dx in range(4) for dy in range(4)}
    return [(on_fx[dz, dc], on_fy[dx, dy]) for dz, dx, dy, dc in STEPS]


def exchange_kernel(
    tracers, dest, slot, diff, flux,
    ue, us,
    tv, dest_v, slot_v, table, table_t, onehot, onehot_own, rank_v,
    matches, picks, chosen, widen, req, req_in, rep, rep_in, dsplit, kv_own, kv, edge_kv, edge_kv_in, kv_halo,
    halo, edge, edge_in, side_raw, side_kv, edge_kv_all, ratio_own, ratio_halo, ratio_side,
    load_sem, tv_sem, req_s, req_r, rep_s, rep_r, row_s, row_r, edge_s, edge_r,
    kvrow_s, kvrow_r, kvedge_s, kvedge_r,
):
    fx, fy = lax.axis_index("fx"), lax.axis_index("fy")
    me = fx * N_FY + fy
    up, down = (fx + N_FX - 1) % N_FX, (fx + 1) % N_FX
    left, right = (fy + N_FY - 1) % N_FY, (fy + 1) % N_FY

    loads = [
        pltpu.make_async_copy(dest, dest_v, load_sem.at[0]),
        pltpu.make_async_copy(slot, slot_v, load_sem.at[1]),
        pltpu.make_async_copy(diff, table.at[pl.ds(0, LEV)], load_sem.at[2]),
        pltpu.make_async_copy(flux, table.at[pl.ds(LEV, TR)], load_sem.at[3]),
    ]
    for load in loads:
        load.start()
    tv_load = pltpu.make_async_copy(tracers, tv, tv_sem)
    tv_load.start()

    barrier = pltpu.get_barrier_semaphore()
    peers = all_peers(fx, fy)

    def each_peer(action):
        for px, py in peers:
            action(px, py)

    def hello(px, py):
        pl.semaphore_signal(barrier, inc=1, device_id=(px, py), device_id_type=MESH)

    each_peer(hello)

    loads[0].wait()
    loads[1].wait()
    lane128 = iota((DEV, CY), 1)
    sub128 = iota((DEV, CY), 0)
    prefix = jnp.concatenate(
        [jnp.where(sub128 < lane128, 1.0, 0.0), jnp.ones((DEV, CY), F32)], 1
    ).astype(BF16)

    kk = iota((16, CY), 0)
    seen = jnp.zeros((DEV, CY), F32)
    for i in range(CX):
        d = dest_v[pl.ds(i, 1), :]
        d = jnp.where(d == me, -1, d)
        slots = slot_v[pl.ds(i, 1), :]
        match = jnp.where(d == sub128, 1.0, 0.0)
        mb = match.astype(BF16)
        matches[:, pl.ds(i * CY, CY)] = mb
        counts = jnp.dot(mb, prefix, preferred_element_type=F32)
        rank = jnp.sum(match * (counts[:, :CY] + seen), axis=0, keepdims=True)
        seen = seen + counts[:, CY:]
        rank_v[pl.ds(i, 1), :] = rank
        value = jnp.where(kk < 8, (slots >> 7) + 1, slots & 127).astype(F32)
        picks[:, pl.ds(i * CY, CY)] = jnp.where((kk & 7).astype(F32) == rank, value, 0.0).astype(BF16)
    asked = lax.dot_general(
        matches[...], picks[...], (((1,), (1,)), ((), ())), preferred_element_type=F32
    )
    req[:, 0, :] = jnp.concatenate([asked, jnp.zeros((DEV, CY - 16), F32)], 1)

    loads[2].wait()
    loads[3].wait()

    def flip(b, carry):
        cols = pl.ds(pl.multiple_of(b * 128, 128), 128)
        part = jnp.concatenate([table[:, cols], jnp.zeros((128 - VALS, 128), F32)], 0)
        hi, lo = split2(part.T)
        table_t[cols, pl.ds(0, 128)] = hi
        table_t[cols, pl.ds(128, 128)] = lo
        return carry

    lax.fori_loop(0, SLOTS // 128, flip, 0)

    for m in range(2 * CAP):
        lane_of = m if m < CAP else 8 + m - CAP
        widen[:, pl.ds(m * CY, CY)] = jnp.where(sub128 == lane_of, 1.0, 0.0).astype(BF16)

    def spread(i, carry):
        cols = pl.ds(pl.multiple_of(i * CY, CY), CY)
        d = dest_v[pl.ds(i, 1), :]
        d = jnp.where(d == me, -1, d)
        rank = rank_v[pl.ds(i, 1), :]
        hit = d == sub128
        for k in range(CAP):
            onehot[pl.ds(k * DEV, DEV), cols] = jnp.where(
                hit & (rank == float(k)), 1.0, 0.0
            ).astype(BF16)
        return carry

    lax.fori_loop(0, CX, spread, 0)
    pl.semaphore_wait(barrier, DEV - 1)

    def ask(px, py):
        pltpu.make_async_remote_copy(
            req.at[px * N_FY + py], req_in.at[me], req_s, req_r,
            device_id=(px, py), device_id_type=MESH,
        ).start()

    each_peer(ask)
    req_in[me] = jnp.zeros((1, CY), F32)

    rows = []
    for t in range(TR):
        rows.append(
            pltpu.make_async_remote_copy(
                tracers.at[t, :, pl.ds(14, 2), :],
                halo.at[:, pl.ds(8 * t + 6, 2), :],
                row_s.at[t], row_r.at[t], device_id=(down, fy), device_id_type=MESH,
            )
        )
        rows.append(
            pltpu.make_async_remote_copy(
                tracers.at[t, :, pl.ds(0, 2), :],
                halo.at[:, pl.ds(8 * t + 8, 2), :],
                row_s.at[TR + t], row_r.at[TR + t], device_id=(up, fy), device_id_type=MESH,
            )
        )
    for copy in rows:
        copy.start()

    tv_load.wait()
    lane16 = iota((CX, CY), 1)

    def pack(q, carry):
        first = last = jnp.zeros((CX, CY), F32)
        for lg in range(8):
            for t in range(TR):
                cells = tv[t, q + 9 * lg]
                at = 16 * lg + 2 * t
                here = (lane16 == at) | (lane16 == at + 1)
                first = jnp.where(here, pltpu.roll(cells, at, 1) if at else cells, first)
                moved = pltpu.roll(cells, (at + 2) % 128, 1) if (at + 2) % 128 else cells
                last = jnp.where(here, moved, last)
        edge[0, q] = last
        edge[1, q] = first
        return carry

    lax.fori_loop(0, 9, pack, 0)

    def to_sides(sources, target, sends, receives):
        places = [
            (fx, right, 0, 0, CX), (fx, left, 1, 0, CX),
            (down, right, 2, CX - 1, 1), (down, left, 3, CX - 1, 1),
            (up, right, 4, 0, 1), (up, left, 5, 0, 1),
        ]
        copies = [
            pltpu.make_async_remote_copy(
                sources[n % 2].at[:, pl.ds(first, count), :],
                target.at[n, :, pl.ds(first, count), :],
                sends.at[n], receives.at[n], device_id=(px, py), device_id_type=MESH,
            )
            for px, py, n, first, count in places
        ]
        for copy in copies:
            copy.start()
        return copies

    edges = to_sides((edge.at[0], edge.at[1]), edge_in, edge_s, edge_r)

    pltpu.make_async_copy(req_in.at[pl.ds(0, DEV - 1)], req_in.at[pl.ds(0, DEV - 1)], req_r).wait()
    wanted = req_in[:, 0, :]
    zero_b = jnp.zeros((DEV, CY), BF16)
    zero_f = jnp.zeros((DEV, CY), F32)
    lane_f = lane128.astype(F32)
    apart = jnp.dot(wanted.astype(BF16), widen[...], preferred_element_type=F32)
    for k in range(CAP):
        high = apart[:, k * CY : (k + 1) * CY].astype(BF16)
        low = jnp.where(apart[:, (CAP + k) * CY : (CAP + k + 1) * CY] == lane_f, 1.0, 0.0).astype(BF16)
        for b in range(SLOTS // 128):
            chosen[pl.ds(k * DEV, DEV), pl.ds(b * 128, 128)] = jnp.where(high == float(b + 1), low, zero_b)
    both = jnp.dot(chosen[...], table_t[...], preferred_element_type=F32)
    both = both[:, :128] + both[:, 128:]
    got = [both[k * DEV : (k + 1) * DEV] for k in range(CAP)]
    for j in range(3):
        rep[:, j, :] = jnp.where(lane128 < 64, got[2 * j], pltpu.roll(got[2 * j + 1], 64, 1))
    tail = jnp.zeros((DEV, CY), F32)
    for k in range(CAP):
        shift = (16 * k - 64) % 128
        moved = pltpu.roll(got[k], shift, 1) if shift else got[k]
        tail = jnp.where(lane128 // 16 == k, moved, tail)
    rep[:, 3, :] = tail

    def answer(px, py):
        pltpu.make_async_remote_copy(
            rep.at[px * N_FY + py], rep_in.at[me], rep_s, rep_r,
            device_id=(px, py), device_id_type=MESH,
        ).start()

    each_peer(answer)
    rep_in[me] = jnp.zeros((4, CY), F32)

    tab3 = jnp.concatenate(split3(table[...]), 0)

    def keep(i, carry):
        for half in range(2):
            d = dest_v[pl.ds(2 * i + half, 1), :]
            s = jnp.where(d == me, slot_v[pl.ds(2 * i + half, 1), :], -1)
            high = ((s >> 7).astype(F32) + zero_f).astype(BF16)
            low = jnp.where((s & 127) == sub128, 1.0, 0.0).astype(BF16)
            for b in range(SLOTS // 128):
                onehot_own[pl.ds(b * 128, 128), pl.ds(half * CY, CY)] = jnp.where(
                    high == float(b), low, zero_b
                )
        three = jnp.dot(tab3, onehot_own[...], preferred_element_type=F32)
        kv_own[:, pl.ds(pl.multiple_of(i * 2 * CY, 2 * CY), 2 * CY)] = (
            three[:VALS] + three[VALS : 2 * VALS] + three[2 * VALS :]
        )
        return carry

    lax.fori_loop(0, CX // 2, keep, 0)

    for copy in edges:
        copy.wait_recv()
    lane8 = iota((8, CY), 1)
    sub8 = iota((8, CY), 0)
    lane24 = iota((24, CY), 1)

    def gather_edges(q, carry):
        def merged(n, rows):
            return edge_in[n + 1, q, rows], edge_in[n, q, rows]

        sides = merged(0, pl.ds(0, CX))
        over = merged(2, pl.ds(8, 8))
        under = merged(4, pl.ds(0, 8))
        right_cells, left_cells = (
            jnp.concatenate([a, jnp.where(sub8 == 7, b, c)], 0)
            for a, b, c in zip(sides, over, under)
        )
        for lg in range(8):
            near_r = pltpu.roll(right_cells, 128 - 16 * lg, 1) if lg else right_cells
            near_l = pltpu.roll(left_cells, (144 - 16 * lg) % 128, 1) if lg != 1 else left_cells
            side_raw[9 * lg + q] = jnp.where(lane24 < 16, near_r, near_l)
        return carry

    lax.fori_loop(0, 9, gather_edges, 0)

    pltpu.make_async_copy(rep_in.at[pl.ds(0, DEV - 1)], rep_in.at[pl.ds(0, DEV - 1)], rep_r).wait()
    last = rep_in[:, 3, :]
    for k in range(CAP):
        main = rep_in[:, k // 2, :]
        if k % 2:
            main = pltpu.roll(main, 64, 1)
        shift = (64 - 16 * k) % 128
        end = pltpu.roll(last, shift, 1) if shift else last
        cols = jnp.where(lane128 < 64, main, jnp.where(lane128 < VALS, end, 0.0))
        hi, lo = split2(cols.T[:VALS])
        dsplit[pl.ds(0, VALS), pl.ds(k * DEV, DEV)] = hi
        dsplit[pl.ds(VALS, VALS), pl.ds(k * DEV, DEV)] = lo

    def assemble(i, carry):
        cols = pl.ds(pl.multiple_of(i * 2 * CY, 2 * CY), 2 * CY)
        two = jnp.dot(dsplit[...], onehot[:, cols], preferred_element_type=F32)
        full = kv_own[:, cols] + two[:VALS] + two[VALS:]
        kv[:, 2 * i, :] = full[:, :CY]
        kv[:, 2 * i + 1, :] = full[:, CY:]
        return carry

    for i in range(CX // 2):
        assemble(i, 0)

    kvrows = [
        pltpu.make_async_remote_copy(
            kv.at[:, pl.ds(14, 2), :], kv_halo.at[:, pl.ds(6, 2), :],
            kvrow_s.at[0], kvrow_r.at[0], device_id=(down, fy), device_id_type=MESH,
        ),
        pltpu.make_async_remote_copy(
            kv.at[:, pl.ds(0, 2), :], kv_halo.at[:, pl.ds(0, 2), :],
            kvrow_s.at[1], kvrow_r.at[1], device_id=(up, fy), device_id_type=MESH,
        ),
    ]
    for copy in kvrows:
        copy.start()
    for g in range(3):
        acc = jnp.zeros((CX, CY), F32)
        for m in range(32 if g < 2 else VALS - 64):
            moved = pltpu.roll(kv[32 * g + m], 4 * m + 2, 1) if 4 * m + 2 < 128 else kv[32 * g + m]
            acc = jnp.where(lane16 // 4 == m, moved, acc)
        edge_kv[g] = acc
    kvedges = to_sides((edge_kv, edge_kv), edge_kv_in, kvedge_s, kvedge_r)

    def factors(kv_above, kv_here, share):
        rest = 1.0 + kv_above * share
        inverse = 1.0 / (rest + kv_here)
        return kv_here * inverse, inverse, rest * inverse

    zero16 = jnp.zeros((CX, CY), F32)
    ones16 = jnp.ones((CX, CY), F32)
    last_level = LEV - 1

    def forward(level, carry):
        above, share, partial = carry
        here = kv[level]
        ratio, inverse, share = factors(above, here, share)
        ratio_own[level] = ratio
        new = []
        for t in range(TR):
            g = (tv[t, level] + above * partial[t]) * inverse
            ue[level, pl.ds(STRIDE * t + 8, CX), :] = g
            new.append(g)
        return here, share, tuple(new)

    above, share, partial = lax.fori_loop(
        0, last_level, forward, (zero16, ones16, (zero16,) * TR)
    )
    _, inverse, _ = factors(above, kv[last_level], share)
    below = []
    for t in range(TR):
        x = (tv[t, last_level] + kv[LEV + t] + above * partial[t]) * inverse
        ue[last_level, pl.ds(STRIDE * t + 8, CX), :] = x
        below.append(x)

    def backward(step, below):
        level = last_level - 1 - step
        ratio = ratio_own[level]
        new = []
        for t in range(TR):
            rows_t = pl.ds(STRIDE * t + 8, CX)
            x = ue[level, rows_t, :] + ratio * below[t]
            ue[level, rows_t, :] = x
            new.append(x)
        return tuple(new)

    lax.fori_loop(0, last_level, backward, tuple(below))

    for copy in kvrows + kvedges:
        copy.wait_recv()
    for copy in rows:
        copy.wait_recv()
    for g in range(3):
        edge_kv_all[g, pl.ds(0, CX), :] = jnp.where(lane16 % 4 < 2, edge_kv_in[0, g], edge_kv_in[1, g])
        over = jnp.where(lane8 % 4 < 2, edge_kv_in[2, g, pl.ds(8, 8)], edge_kv_in[3, g, pl.ds(8, 8)])
        under = jnp.where(lane8 % 4 < 2, edge_kv_in[4, g, pl.ds(0, 8)], edge_kv_in[5, g, pl.ds(0, 8)])
        edge_kv_all[g, pl.ds(CX, 8), :] = jnp.where(sub8 == 7, over, under)
    quad = jnp.where(lane24 % 32 < 16, 2, 0) + lane24 % 2

    for level in range(LEV):
        side_kv[level] = jnp.take_along_axis(
            edge_kv_all[level // 32], 4 * (level % 32) + quad, axis=1
        )

    side_flux = jnp.take_along_axis(
        edge_kv_all[2], 32 + 4 * ((lane24 % 16) // 2) + quad, axis=1
    )

    def forward_rim(level, carry):
        above, share, partial, sabove, sshare, spartial = carry
        here = kv_halo[level]
        ratio, inverse, share = factors(above, here, share)
        ratio_halo[level] = ratio
        new = []
        for j in range(TR + 1):
            g = (halo[level, pl.ds(8 * j, 8), :] + above * partial[j]) * inverse
            ue[level, pl.ds(STRIDE * j, 8), :] = g
            new.append(g)
        shere = side_kv[level]
        ratio, inverse, sshare = factors(sabove, shere, sshare)
        ratio_side[level] = ratio
        g = (side_raw[level] + sabove * spartial) * inverse
        us[level, pl.ds(8, 24), :] = g
        return here, share, tuple(new), shere, sshare, g

    zero8 = jnp.zeros((8, CY), F32)
    zero24 = jnp.zeros((24, CY), F32)
    above, share, partial, sabove, sshare, spartial = lax.fori_loop(
        0, last_level, forward_rim,
        (zero8, zero8 + 1.0, (zero8,) * (TR + 1), zero24, zero24 + 1.0, zero24),
    )
    _, inverse, _ = factors(above, kv_halo[last_level], share)
    below = []
    for j in range(TR + 1):
        source = jnp.where(
            sub8 < 4, kv_halo[LEV + max(j - 1, 0)], kv_halo[LEV + min(j, TR - 1)]
        )
        x = (halo[last_level, pl.ds(8 * j, 8), :] + source + above * partial[j]) * inverse
        ue[last_level, pl.ds(STRIDE * j, 8), :] = x
        below.append(x)
    _, inverse, _ = factors(sabove, side_kv[last_level], sshare)
    sbelow = (side_raw[last_level] + side_flux + sabove * spartial) * inverse
    us[last_level, pl.ds(8, 24), :] = sbelow
    us[last_level, pl.ds(0, 8), :] = sbelow[16:24]

    def backward_rim(step, carry):
        level = last_level - 1 - step
        below, sbelow = carry
        ratio = ratio_halo[level]
        new = []
        for j in range(TR + 1):
            rows_j = pl.ds(STRIDE * j, 8)
            x = ue[level, rows_j, :] + ratio * below[j]
            ue[level, rows_j, :] = x
            new.append(x)
        x = us[level, pl.ds(8, 24), :] + ratio_side[level] * sbelow
        us[level, pl.ds(8, 24), :] = x
        us[level, pl.ds(0, 8), :] = x[16:24]
        return tuple(new), x

    lax.fori_loop(0, last_level, backward_rim, (tuple(below), sbelow))

    for copy in rows + edges + kvrows + kvedges:
        copy.wait_send()
    pltpu.make_async_copy(req.at[pl.ds(0, DEV - 1)], req.at[pl.ds(0, DEV - 1)], req_s).wait()
    pltpu.make_async_copy(rep.at[pl.ds(0, DEV - 1)], rep.at[pl.ds(0, DEV - 1)], rep_s).wait()


def smooth_kernel(ue, us, out, parts, weights, side_weights, side_out):
    block, blocks = pl.program_id(0), pl.num_programs(0)
    count = out.shape[1]
    held = count * CX
    lane = iota((held, CY), 1)

    def sides(at, into):
        levels = pl.ds(at * count, count)

        def cells(first):
            return us[levels, pl.ds(first, CX), :].reshape(held, CY)

        u = cells(8)
        q = 2.0 * (cells(7) + cells(9)) - 8.0 * u
        across = jnp.where(
            lane < 16,
            jnp.where(lane % 2 == 1, pltpu.roll(q, 1, 1), 0.0),
            jnp.where(lane % 2 == 0, pltpu.roll(q, CY - 1, 1), 0.0),
        )
        side = u + across
        rest = side - side.astype(BF16).astype(F32)
        both = jnp.where(lane < 32, side, jnp.where(lane < 64, pltpu.roll(rest, 32, 1), 0.0))
        side_out[into] = jnp.dot(both.astype(BF16), side_weights[...], preferred_element_type=F32)

    @pl.when(block == 0)
    def _():
        gap = jnp.abs(iota((CY, CY), 0) - iota((CY, CY), 1))
        first = jnp.where(gap == 0, 20.0, jnp.where(gap == 1, -8.0, jnp.where(gap == 2, 1.0, 0.0)))
        second = jnp.where(gap == 0, -8.0, jnp.where(gap == 1, 2.0, 0.0))
        for n, part in enumerate((first, first, second, second)):
            weights[pl.ds(n * CY, CY), :] = part.astype(BF16)
        row, col = iota((CY, CY), 0), iota((CY, CY), 1)
        goal = (row % 32) // 16 * 2 + row % 2
        for t in range(TR):
            hit = (row < 64) & ((row % 16) // 2 == t) & (col == (goal + CY - 2) % CY)
            side_weights[:, pl.ds(t * CY, CY)] = jnp.where(hit, 1.0, 0.0).astype(BF16)
        sides(0, 0)

    side_now = block % 2
    for n in range(count):
        level = block * count + n
        for t in range(TR):
            row = STRIDE * t + 8
            u = ue[level, pl.ds(row, CX), :]
            near = ue[level, pl.ds(row - 1, CX), :] + ue[level, pl.ds(row + 1, CX), :]
            for m, part in enumerate(split2(u) + split2(near)):
                parts[pl.ds((n * TR + t) * CX, CX), pl.ds(m * CY, CY)] = part
    mixed = jnp.dot(parts[...], weights[...], preferred_element_type=F32)
    for n in range(count):
        level = block * count + n
        for t in range(TR):
            row = STRIDE * t + 8
            u = ue[level, pl.ds(row, CX), :]
            far = ue[level, pl.ds(row - 2, CX), :] + ue[level, pl.ds(row + 2, CX), :]
            edge = side_out[side_now, pl.ds(n * CX, CX), pl.ds(t * CY, CY)]
            at = (n * TR + t) * CX
            out[t, n] = u - 0.025 * (far + edge + mixed[at : at + CX])
    sides(jnp.minimum(block + 1, blocks - 1), 1 - side_now)


def local(tracers, group_dest, group_slot, diffusivity, surface_flux):
    any_spec = pl.BlockSpec(memory_space=pltpu.HBM)
    dma = pltpu.SemaphoreType.DMA
    ue, us = pl.pallas_call(
        exchange_kernel,
        out_shape=(
            pltpu.VMEM((LEV, UROWS, CY), F32),
            pltpu.VMEM((LEV, 32, CY), F32),
        ),
        in_specs=[any_spec] * 5,
        out_specs=(pl.BlockSpec(memory_space=pltpu.VMEM), pl.BlockSpec(memory_space=pltpu.VMEM)),
        scratch_shapes=[
            pltpu.VMEM((TR, LEV, CX, CY), F32),
            pltpu.VMEM((CX, CY), jnp.int32),
            pltpu.VMEM((CX, CY), jnp.int32),
            pltpu.VMEM((VALS, SLOTS), F32),
            pltpu.VMEM((SLOTS, 256), BF16),
            pltpu.VMEM((CAP * DEV, SLOTS), BF16),
            pltpu.VMEM((SLOTS, 256), BF16),
            pltpu.VMEM((CX, CY), F32),
            pltpu.VMEM((DEV, SLOTS), BF16),
            pltpu.VMEM((16, SLOTS), BF16),
            pltpu.VMEM((CAP * DEV, SLOTS), BF16),
            pltpu.VMEM((DEV, 2 * CAP * CY), BF16),
            pltpu.VMEM((DEV, 1, CY), F32),
            pltpu.VMEM((DEV, 1, CY), F32),
            pltpu.VMEM((DEV, 4, CY), F32),
            pltpu.VMEM((DEV, 4, CY), F32),
            pltpu.VMEM((2 * VALS, CAP * DEV), BF16),
            pltpu.VMEM((VALS, SLOTS), F32),
            pltpu.VMEM((VALS, CX, CY), F32),
            pltpu.VMEM((3, CX, CY), F32),
            pltpu.VMEM((6, 3, CX, CY), F32),
            pltpu.VMEM((VALS, 8, CY), F32),
            pltpu.VMEM((LEV, 8 * (TR + 1), CY), F32),
            pltpu.VMEM((2, 9, CX, CY), F32),
            pltpu.VMEM((6, 9, CX, CY), F32),
            pltpu.VMEM((LEV, 24, CY), F32),
            pltpu.VMEM((LEV, 24, CY), F32),
            pltpu.VMEM((3, 24, CY), F32),
            pltpu.VMEM((LEV, CX, CY), F32),
            pltpu.VMEM((LEV, 8, CY), F32),
            pltpu.VMEM((LEV, 24, CY), F32),
            dma((4,)), dma, dma, dma, dma, dma,
            dma((2 * TR,)), dma((2 * TR,)), dma((6,)), dma((6,)),
            dma((2,)), dma((2,)), dma((6,)), dma((6,)),
        ],
        compiler_params=pltpu.CompilerParams(
            collective_id=0, has_side_effects=True, vmem_limit_bytes=44 << 20
        ),
        name="exchange",
    )(
        *(
            pltpu.with_memory_space_constraint(x, pltpu.HBM)
            for x in (tracers, group_dest, group_slot, diffusivity, surface_flux)
        )
    )
    count = 9
    whole = pl.BlockSpec(memory_space=pltpu.VMEM)
    return pl.pallas_call(
        smooth_kernel,
        grid=(LEV // count,),
        out_shape=jax.ShapeDtypeStruct(tracers.shape, F32),
        in_specs=[whole, whole],
        out_specs=pl.BlockSpec((TR, count, CX, CY), lambda b: (0, b, 0, 0)),
        scratch_shapes=[
            pltpu.VMEM((count * TR * CX, 4 * CY), BF16),
            pltpu.VMEM((4 * CY, CY), BF16),
            pltpu.VMEM((CY, TR * CY), BF16),
            pltpu.VMEM((2, count * CX, TR * CY), F32),
        ],
        compiler_params=pltpu.CompilerParams(vmem_limit_bytes=20 << 20),
        name="smooth",
    )(ue, us)


def solution(mesh):
    placed = (
        P(None, None, "fx", "fy"),
        P("fx", "fy"),
        P("fx", "fy"),
        P(None, ("fx", "fy")),
        P(None, ("fx", "fy")),
    )
    return jax.shard_map(
        local, mesh=mesh, in_specs=placed, out_specs=P(None, None, "fx", "fy"), check_vma=False
    )
```

time: 77.7 us -> 40 us (0.51)
  Pallas kernels: 74.2 us -> 39.8 us
  local copies, waits for them, and re-layouts: 3.3 us -> 0 us
    pallas_call x1, Pallas kernels: 59.1 us -> 33.2 us  [local(): pl.pallas_call(exchange_kernel, out_shape=(pltpu.VMEM((LEV, UROWS, CY), F...]
    pallas_call x1, Pallas kernels: 15.1 us -> 6.59 us  [local(): pl.pallas_call(smooth_kernel, grid=(LEV // count,), out_shape=jax.ShapeDt...]
    unnamed x8 -> x0, local copies, waits for them, and re-layouts: 3.3 us -> none
where the time goes in v2:
time: 40 us; the launch traced here: 39.8 us
  Pallas kernels  39.8 us (99%)
    pallas_call x1, Pallas kernels, local(): pl.pallas_call(exchange_kernel, out_shape=(pltpu.VMEM((LEV, UROWS, CY), F...  33.2 us
    pallas_call x1, Pallas kernels, local(): pl.pallas_call(smooth_kernel, grid=(LEV // count,), out_shape=jax.ShapeDt...  6.59 us

profile of v2, /device:TPU:1, one launch (start us, length us, event | category | flops | bytes accessed | tf_op | source)
XLA Modules:
  0.0 39.8 jit_solution(6452446932362665781)
XLA Ops:
  0.0 33.2 %exchange.1 = (f32[72,200,128]{2,1,0:T(8,128)S(1)}, f32[72,32,128]{2,1,0:T(8,128)S(1)}) custom-call(f32[8,72,16,128]{3,2,1,0:T(8,128)} %tracers.1, s32[16,128]{1,0:T(8,128)} %dest.1, s32[16,128]{1,0:T(8,128)} %slot.1, f32[72,2048]{1,0:T(8,128)} %diff.1, f32[8,2048]{1,0:T(8,128)} %flux.1), custom_call_target="tpu_custom_call" | custom-call | tf_op jit(solution)/shard_map/exchange/pallas_call | solution.py:530
  33.2 6.6 %smooth.1 = f32[8,72,16,128]{3,2,1,0:T(8,128)} custom-call(f32[72,200,128]{2,1,0:T(8,128)S(1)} %get-tuple-element.7.ue, f32[72,32,128]{2,1,0:T(8,128)S(1)} %get-tuple-element.8.us), custom_call_target="tpu_custom_call" | custom-call | tf_op jit(solution)/shard_map/smooth/pallas_call | solution.py:586

commit v3 on v2

--- a/solution.py
+++ b/solution.py
@@ -57,10 +57,10 @@
 
 def exchange_kernel(
     tracers, dest, slot, diff, flux,
-    ue, us,
+    ue, us, ua, ub,
     tv, dest_v, slot_v, table, table_t, onehot, onehot_own, rank_v,
     matches, picks, chosen, widen, req, req_in, rep, rep_in, dsplit, kv_own, kv, edge_kv, edge_kv_in, kv_halo,
-    halo, edge, edge_in, side_raw, side_kv, edge_kv_all, ratio_own, ratio_halo, ratio_side,
+    halo, edge, edge_in, side_raw, side_kv, edge_kv_all, ratio_own, ratio_halo, ratio_side, parts, weights,
     load_sem, tv_sem, req_s, req_r, rep_s, rep_r, row_s, row_r, edge_s, edge_r,
     kvrow_s, kvrow_r, kvedge_s, kvedge_r,
 ):
@@ -218,6 +218,13 @@
         return copies
 
     edges = to_sides((edge.at[0], edge.at[1]), edge_in, edge_s, edge_r)
+
+    gap = jnp.abs(sub128 - lane128)
+    first = jnp.where(gap == 0, 20.0, jnp.where(gap == 1, -8.0, jnp.where(gap == 2, 1.0, 0.0)))
+    second = jnp.where(gap == 0, -8.0, jnp.where(gap == 1, 2.0, 0.0))
+    for n in range(2):
+        weights[pl.ds(n * CY, CY), pl.ds(0, CY)] = first.astype(BF16)
+        weights[pl.ds(n * CY, CY), pl.ds(CY, CY)] = second.astype(BF16)
 
     pltpu.make_async_copy(req_in.at[pl.ds(0, DEV - 1)], req_in.at[pl.ds(0, DEV - 1)], req_r).wait()
     wanted = req_in[:, 0, :]
@@ -340,49 +347,98 @@
         edge_kv[g] = acc
     kvedges = to_sides((edge_kv, edge_kv), edge_kv_in, kvedge_s, kvedge_r)
 
-    def factors(kv_above, kv_here, share):
-        rest = 1.0 + kv_above * share
-        inverse = 1.0 / (rest + kv_here)
-        return kv_here * inverse, inverse, rest * inverse
-
-    zero16 = jnp.zeros((CX, CY), F32)
-    ones16 = jnp.ones((CX, CY), F32)
-    last_level = LEV - 1
-
-    def forward(level, carry):
-        above, share, partial = carry
-        here = kv[level]
-        ratio, inverse, share = factors(above, here, share)
-        ratio_own[level] = ratio
-        new = []
-        for t in range(TR):
-            g = (tv[t, level] + above * partial[t]) * inverse
-            ue[level, pl.ds(STRIDE * t + 8, CX), :] = g
-            new.append(g)
-        return here, share, tuple(new)
-
-    above, share, partial = lax.fori_loop(
-        0, last_level, forward, (zero16, ones16, (zero16,) * TR)
-    )
-    _, inverse, _ = factors(above, kv[last_level], share)
-    below = []
+    def factors(before, after, share):
+        rest = 1.0 + before * share
+        inverse = 1.0 / (rest + after)
+        return after * inverse, inverse, rest * inverse
+
+    def solve(*systems):
+        def inwards(step, carry):
+            done = []
+            for (coupling, ratios, right_sides, count, put, _), state in zip(systems, carry):
+                for (before, share, partial), level, nearer in zip(
+                    state, (step, LEV - 1 - step), (step, LEV - 2 - step)
+                ):
+                    after = coupling[nearer]
+                    ratio, inverse, share = factors(before, after, share)
+                    ratios[level] = ratio
+                    new = []
+                    for j in range(count):
+                        g = (right_sides(level, j) + before * partial[j]) * inverse
+                        put(level, j, g)
+                        new.append(g)
+                    done.append((after, share, tuple(new)))
+            return tuple(zip(done[0::2], done[1::2]))
+
+        start = []
+        for coupling, _, _, count, _, _ in systems:
+            last = coupling[LEV - 1]
+            zero = jnp.zeros_like(last)
+            zeros = (zero,) * count
+            start.append(((zero, zero + 1.0, zeros), (last, zero + 1.0, zeros)))
+        met = lax.fori_loop(0, LEV // 2, inwards, tuple(start))
+        high, low = LEV // 2 - 1, LEV // 2
+        ends = []
+        for (_, ratios, _, count, put, _), ((_, _, top), (_, _, bottom)) in zip(systems, met):
+            e, f = ratios[high], ratios[low]
+            scale = 1.0 / (1.0 - e * f)
+            above, below = [], []
+            for j in range(count):
+                x = (top[j] + e * bottom[j]) * scale
+                y = bottom[j] + f * x
+                put(high, j, x)
+                put(low, j, y)
+                above.append(x)
+                below.append(y)
+            ends.append((tuple(above), tuple(below)))
+
+        def outwards(step, carry):
+            done = []
+            for (_, ratios, _, count, put, get), state in zip(systems, carry):
+                for last, level in zip(state, (high - 1 - step, low + 1 + step)):
+                    ratio = ratios[level]
+                    new = []
+                    for j in range(count):
+                        x = get(level, j) + ratio * last[j]
+                        put(level, j, x)
+                        new.append(x)
+                    done.append(tuple(new))
+            return tuple(zip(done[0::2], done[1::2]))
+
+        lax.fori_loop(0, LEV // 2 - 1, outwards, tuple(ends))
+
     for t in range(TR):
-        x = (tv[t, last_level] + kv[LEV + t] + above * partial[t]) * inverse
-        ue[last_level, pl.ds(STRIDE * t + 8, CX), :] = x
-        below.append(x)
-
-    def backward(step, below):
-        level = last_level - 1 - step
-        ratio = ratio_own[level]
-        new = []
-        for t in range(TR):
-            rows_t = pl.ds(STRIDE * t + 8, CX)
-            x = ue[level, rows_t, :] + ratio * below[t]
-            ue[level, rows_t, :] = x
-            new.append(x)
-        return tuple(new)
-
-    lax.fori_loop(0, last_level, backward, tuple(below))
+        tv[t, LEV - 1] = tv[t, LEV - 1] + kv[LEV + t]
+
+    def put_own(level, t, x):
+        ue[level, pl.ds(STRIDE * t + 8, CX), :] = x
+
+    solve(
+        (kv, ratio_own, lambda level, t: tv[t, level], TR, put_own,
+         lambda level, t: ue[level, pl.ds(STRIDE * t + 8, CX), :])
+    )
+
+    def mix(b, carry):
+        group = 9
+        for n in range(group):
+            for t in range(TR):
+                at = pl.ds((n * TR + t) * CX, CX)
+                hi, lo = split2(ue[b * group + n, pl.ds(STRIDE * t + 8, CX), :])
+                parts[at, pl.ds(0, CY)] = hi
+                parts[at, pl.ds(CY, CY)] = lo
+        mixed = jnp.dot(parts[...], weights[...], preferred_element_type=F32)
+        for n in range(group):
+            for t in range(TR):
+                own = pl.ds(STRIDE * t + 8, CX)
+                at = (n * TR + t) * CX
+                both = mixed[at : at + CX]
+                ua[b * group + n, pl.ds(t * CX, CX), :] = (
+                    ue[b * group + n, own, :] - 0.025 * both[:, :CY]
+                )
+                ub[b * group + n, own, :] = both[:, CY:]
+        return carry
+
+    lax.fori_loop(0, LEV // 9, mix, 0)
 
     for copy in kvrows + kvedges:
         copy.wait_recv()
@@ -404,59 +460,39 @@
         edge_kv_all[2], 32 + 4 * ((lane24 % 16) // 2) + quad, axis=1
     )
 
-    def forward_rim(level, carry):
-        above, share, partial, sabove, sshare, spartial = carry
-        here = kv_halo[level]
-        ratio, inverse, share = factors(above, here, share)
-        ratio_halo[level] = ratio
-        new = []
-        for j in range(TR + 1):
-            g = (halo[level, pl.ds(8 * j, 8), :] + above * partial[j]) * inverse
-            ue[level, pl.ds(STRIDE * j, 8), :] = g
-            new.append(g)
-        shere = side_kv[level]
-        ratio, inverse, sshare = factors(sabove, shere, sshare)
-        ratio_side[level] = ratio
-        g = (side_raw[level] + sabove * spartial) * inverse
-        us[level, pl.ds(8, 24), :] = g
-        return here, share, tuple(new), shere, sshare, g
-
-    zero8 = jnp.zeros((8, CY), F32)
-    zero24 = jnp.zeros((24, CY), F32)
-    above, share, partial, sabove, sshare, spartial = lax.fori_loop(
-        0, last_level, forward_rim,
-        (zero8, zero8 + 1.0, (zero8,) * (TR + 1), zero24, zero24 + 1.0, zero24),
-    )
-    _, inverse, _ = factors(above, kv_halo[last_level], share)
-    below = []
     for j in range(TR + 1):
-        source = jnp.where(
+        tile = pl.ds(8 * j, 8)
+        halo[LEV - 1, tile, :] = halo[LEV - 1, tile, :] + jnp.where(
             sub8 < 4, kv_halo[LEV + max(j - 1, 0)], kv_halo[LEV + min(j, TR - 1)]
         )
-        x = (halo[last_level, pl.ds(8 * j, 8), :] + source + above * partial[j]) * inverse
-        ue[last_level, pl.ds(STRIDE * j, 8), :] = x
-        below.append(x)
-    _, inverse, _ = factors(sabove, side_kv[last_level], sshare)
-    sbelow = (side_raw[last_level] + side_flux + sabove * spartial) * inverse
-    us[last_level, pl.ds(8, 24), :] = sbelow
-    us[last_level, pl.ds(0, 8), :] = sbelow[16:24]
-
-    def backward_rim(step, carry):
-        level = last_level - 1 - step
-        below, sbelow = carry
-        ratio = ratio_halo[level]
-        new = []
-        for j in range(TR + 1):
-            rows_j = pl.ds(STRIDE * j, 8)
-            x = ue[level, rows_j, :] + ratio * below[j]
-            ue[level, rows_j, :] = x
-            new.append(x)
-        x = us[level, pl.ds(8, 24), :] + ratio_side[level] * sbelow
+    side_raw[LEV - 1] = side_raw[LEV - 1] + side_flux
+
+    def put_rows(level, j, x):
+        ue[level, pl.ds(STRIDE * j, 8), :] = x
+
+    def put_side(level, j, x):
         us[level, pl.ds(8, 24), :] = x
-        us[level, pl.ds(0, 8), :] = x[16:24]
-        return tuple(new), x
-
-    lax.fori_loop(0, last_level, backward_rim, (tuple(below), sbelow))
+        us[level, pl.ds(0, 8), :] = x[CX:]
+
+    solve(
+        (kv_halo, ratio_halo, lambda level, j: halo[level, pl.ds(8 * j, 8), :], TR + 1, put_rows,
+         lambda level, j: ue[level, pl.ds(STRIDE * j, 8), :]),
+        (side_kv, ratio_side, lambda level, j: side_raw[level], 1, put_side,
+         lambda level, j: us[level, pl.ds(8, 24), :]),
+    )
+
+    for level in range(LEV):
+        rim = jnp.concatenate(
+            [ue[level, pl.ds(7, TR, stride=STRIDE), :], ue[level, pl.ds(STRIDE, TR, stride=STRIDE), :]], 0
+        )
+        hi, lo = split2(rim)
+        parts[pl.ds(level * 2 * TR, 2 * TR), pl.ds(0, CY)] = hi
+        parts[pl.ds(level * 2 * TR, 2 * TR), pl.ds(CY, CY)] = lo
+    fixed = jnp.dot(parts[...], weights[:, pl.ds(CY, CY)], preferred_element_type=F32)
+    for level in range(LEV):
+        at = level * 2 * TR
+        ub[level, pl.ds(7, TR, stride=STRIDE), :] = fixed[at : at + TR]
+        ub[level, pl.ds(STRIDE, TR, stride=STRIDE), :] = fixed[at + TR : at + 2 * TR]
 
     for copy in rows + edges + kvrows + kvedges:
         copy.wait_send()
@@ -464,77 +500,60 @@
     pltpu.make_async_copy(rep.at[pl.ds(0, DEV - 1)], rep.at[pl.ds(0, DEV - 1)], rep_s).wait()
 
 
-def smooth_kernel(ue, us, out, parts, weights, side_weights, side_out):
-    block, blocks = pl.program_id(0), pl.num_programs(0)
-    count = out.shape[1]
-    held = count * CX
-    lane = iota((held, CY), 1)
-
-    def sides(at, into):
-        levels = pl.ds(at * count, count)
-
-        def cells(first):
-            return us[levels, pl.ds(first, CX), :].reshape(held, CY)
-
-        u = cells(8)
-        q = 2.0 * (cells(7) + cells(9)) - 8.0 * u
-        across = jnp.where(
-            lane < 16,
-            jnp.where(lane % 2 == 1, pltpu.roll(q, 1, 1), 0.0),
-            jnp.where(lane % 2 == 0, pltpu.roll(q, CY - 1, 1), 0.0),
-        )
-        side = u + across
-        rest = side - side.astype(BF16).astype(F32)
-        both = jnp.where(lane < 32, side, jnp.where(lane < 64, pltpu.roll(rest, 32, 1), 0.0))
-        side_out[into] = jnp.dot(both.astype(BF16), side_weights[...], preferred_element_type=F32)
-
-    @pl.when(block == 0)
-    def _():
-        gap = jnp.abs(iota((CY, CY), 0) - iota((CY, CY), 1))
-        first = jnp.where(gap == 0, 20.0, jnp.where(gap == 1, -8.0, jnp.where(gap == 2, 1.0, 0.0)))
-        second = jnp.where(gap == 0, -8.0, jnp.where(gap == 1, 2.0, 0.0))
-        for n, part in enumerate((first, first, second, second)):
-            weights[pl.ds(n * CY, CY), :] = part.astype(BF16)
-        row, col = iota((CY, CY), 0), iota((CY, CY), 1)
-        goal = (row % 32) // 16 * 2 + row % 2
-        for t in range(TR):
-            hit = (row < 64) & ((row % 16) // 2 == t) & (col == (goal + CY - 2) % CY)
-            side_weights[:, pl.ds(t * CY, CY)] = jnp.where(hit, 1.0, 0.0).astype(BF16)
-        sides(0, 0)
-
-    side_now = block % 2
-    for n in range(count):
-        level = block * count + n
-        for t in range(TR):
-            row = STRIDE * t + 8
-            u = ue[level, pl.ds(row, CX), :]
-            near = ue[level, pl.ds(row - 1, CX), :] + ue[level, pl.ds(row + 1, CX), :]
-            for m, part in enumerate(split2(u) + split2(near)):
-                parts[pl.ds((n * TR + t) * CX, CX), pl.ds(m * CY, CY)] = part
-    mixed = jnp.dot(parts[...], weights[...], preferred_element_type=F32)
-    for n in range(count):
-        level = block * count + n
-        for t in range(TR):
-            row = STRIDE * t + 8
-            u = ue[level, pl.ds(row, CX), :]
-            far = ue[level, pl.ds(row - 2, CX), :] + ue[level, pl.ds(row + 2, CX), :]
-            edge = side_out[side_now, pl.ds(n * CX, CX), pl.ds(t * CY, CY)]
-            at = (n * TR + t) * CX
-            out[t, n] = u - 0.025 * (far + edge + mixed[at : at + CX])
-    sides(jnp.minimum(block + 1, blocks - 1), 1 - side_now)
+def smooth_kernel(ue, us, ua, ub, out, held, side_weights, side_out, sem):
+    row, col = iota((CY, CY), 0), iota((CY, CY), 1)
+    goal = (row % 32) // 16 * 2 + row % 2
+    for t in range(TR):
+        hit = (row < 64) & ((row % 16) // 2 == t) & (col == (goal + CY - 2) % CY)
+        side_weights[:, pl.ds(t * CY, CY)] = jnp.where(hit, 1.0, 0.0).astype(BF16)
+
+    def cells(first):
+        return us[:, pl.ds(first, CX), :].reshape(LEV * CX, CY)
+
+    lane = iota((LEV * CX, CY), 1)
+    u = cells(8)
+    q = 2.0 * (cells(7) + cells(9)) - 8.0 * u
+    across = jnp.where(
+        lane < 16,
+        jnp.where(lane % 2 == 1, pltpu.roll(q, 1, 1), 0.0),
+        jnp.where(lane % 2 == 0, pltpu.roll(q, CY - 1, 1), 0.0),
+    )
+    side = u + across
+    rest = side - side.astype(BF16).astype(F32)
+    both = jnp.where(lane < 32, side, jnp.where(lane < 64, pltpu.roll(rest, 32, 1), 0.0))
+    side_out[...] = jnp.dot(both.astype(BF16), side_weights[...], preferred_element_type=F32)
+
+    count = 9
+    copies = []
+    for block in range(LEV // count):
+        for level in range(block * count, (block + 1) * count):
+            for t in range(TR):
+                row = STRIDE * t + 8
+                near = ub[level, pl.ds(row - 1, CX), :] + ub[level, pl.ds(row + 1, CX), :]
+                far = ue[level, pl.ds(row - 2, CX), :] + ue[level, pl.ds(row + 2, CX), :]
+                edge = side_out[pl.ds(level * CX, CX), pl.ds(t * CY, CY)]
+                held[t, level] = ua[level, pl.ds(t * CX, CX), :] - 0.025 * ((far + near) + edge)
+        levels = pl.ds(block * count, count)
+        copy = pltpu.make_async_copy(held.at[:, levels], out.at[:, levels], sem.at[block])
+        copy.start()
+        copies.append(copy)
+    for copy in copies:
+        copy.wait()
 
 
 def local(tracers, group_dest, group_slot, diffusivity, surface_flux):
     any_spec = pl.BlockSpec(memory_space=pltpu.HBM)
     dma = pltpu.SemaphoreType.DMA
-    ue, us = pl.pallas_call(
+    ue, us, ua, ub = pl.pallas_call(
         exchange_kernel,
         out_shape=(
             pltpu.VMEM((LEV, UROWS, CY), F32),
             pltpu.VMEM((LEV, 32, CY), F32),
+            pltpu.VMEM((LEV, TR * CX, CY), F32),
+            pltpu.VMEM((LEV, UROWS, CY), F32),
         ),
         in_specs=[any_spec] * 5,
-        out_specs=(pl.BlockSpec(memory_space=pltpu.VMEM), pl.BlockSpec(memory_space=pltpu.VMEM)),
+        out_specs=(pl.BlockSpec(memory_space=pltpu.VMEM),) * 4,
         scratch_shapes=[
             pltpu.VMEM((TR, LEV, CX, CY), F32),
             pltpu.VMEM((CX, CY), jnp.int32),
@@ -567,12 +586,14 @@
             pltpu.VMEM((LEV, CX, CY), F32),
             pltpu.VMEM((LEV, 8, CY), F32),
             pltpu.VMEM((LEV, 24, CY), F32),
+            pltpu.VMEM((9 * TR * CX, 2 * CY), BF16),
+            pltpu.VMEM((2 * CY, 2 * CY), BF16),
             dma((4,)), dma, dma, dma, dma, dma,
             dma((2 * TR,)), dma((2 * TR,)), dma((6,)), dma((6,)),
             dma((2,)), dma((2,)), dma((6,)), dma((6,)),
         ],
         compiler_params=pltpu.CompilerParams(
-            collective_id=0, has_side_effects=True, vmem_limit_bytes=44 << 20
+            collective_id=0, has_side_effects=True, vmem_limit_bytes=30 << 20
         ),
         name="exchange",
     )(
@@ -581,23 +602,21 @@
             for x in (tracers, group_dest, group_slot, diffusivity, surface_flux)
         )
     )
-    count = 9
     whole = pl.BlockSpec(memory_space=pltpu.VMEM)
     return pl.pallas_call(
         smooth_kernel,
-        grid=(LEV // count,),
         out_shape=jax.ShapeDtypeStruct(tracers.shape, F32),
-        in_specs=[whole, whole],
-        out_specs=pl.BlockSpec((TR, count, CX, CY), lambda b: (0, b, 0, 0)),
+        in_specs=[whole] * 4,
+        out_specs=pl.BlockSpec(memory_space=pl.ANY),
         scratch_shapes=[
-            pltpu.VMEM((count * TR * CX, 4 * CY), BF16),
-            pltpu.VMEM((4 * CY, CY), BF16),
+            pltpu.VMEM((TR, LEV, CX, CY), F32),
             pltpu.VMEM((CY, TR * CY), BF16),
-            pltpu.VMEM((2, count * CX, TR * CY), F32),
+            pltpu.VMEM((LEV * CX, TR * CY), F32),
+            dma((8,)),
         ],
-        compiler_params=pltpu.CompilerParams(vmem_limit_bytes=20 << 20),
+        compiler_params=pltpu.CompilerParams(vmem_limit_bytes=16 << 20),
         name="smooth",
-    )(ue, us)
+    )(ue, us, ua, ub)
 
 
 def solution(mesh):

time: 40 us -> 37.1 us (0.927)
  Pallas kernels: 39.8 us -> 36.9 us
    pallas_call x1, Pallas kernels: 6.59 us -> 3.53 us  [local(): pl.pallas_call(smooth_kernel, out_shape=jax.ShapeDtypeStruct(tracers.shap...]
where the time goes in v3:
time: 37.1 us; the launch traced here: 36.9 us
  Pallas kernels  36.9 us (99%)
    pallas_call x1, Pallas kernels, local(): pl.pallas_call(exchange_kernel, out_shape=(pltpu.VMEM((LEV, UROWS, CY), F...  33.3 us
    pallas_call x1, Pallas kernels, local(): pl.pallas_call(smooth_kernel, out_shape=jax.ShapeDtypeStruct(tracers.shap...  3.53 us

profile of v3, /device:TPU:1, one launch (start us, length us, event | category | flops | bytes accessed | tf_op | source)
XLA Modules:
  0.0 36.9 jit_solution(6934051688652928484)
XLA Ops:
  0.0 33.3 %exchange.1 = (f32[72,200,128]{2,1,0:T(8,128)S(1)}, f32[72,32,128]{2,1,0:T(8,128)S(1)}, f32[72,128,128]{2,1,0:T(8,128)S(1)}, f32[72,200,128]{2,1,0:T(8,128)S(1)}) custom-call(f32[8,72,16,128]{3,2,1,0:T(8,128)} %tracers.1, s32[16,128]{1,0:T(8,128)} %dest.1, s32[16,128]{1,0:T(8,128)} %slot.1, f32[72,2048]{1,0:T(8,128)} %diff.1, f32[8,2048]{1,0:T(8,128)} %flux.1), custom_call_target="tpu_custom_call" | custom-call | tf_op jit(solution)/shard_map/exchange/pallas_call | solution.py:547
  33.3 3.5 %smooth.1 = f32[8,72,16,128]{3,2,1,0:T(8,128)} custom-call(f32[72,200,128]{2,1,0:T(8,128)S(1)} %get-tuple-element.9.ue, f32[72,32,128]{2,1,0:T(8,128)S(1)} %get-tuple-element.10.us, f32[72,128,128]{2,1,0:T(8,128)S(1)} %get-tuple-element.11.ua, f32[72,200,128]{2,1,0:T(8,128)S(1)} %get-tuple-element.12.ub), custom_call_target="tpu_custom_call" | custom-call | tf_op jit(solution)/shard_map/smooth/pallas_call | solution.py:606

commit v4 on v3

--- a/solution.py
+++ b/solution.py
@@ -57,8 +57,8 @@
 
 def exchange_kernel(
     tracers, dest, slot, diff, flux,
-    ue, us, ua, ub,
-    tv, dest_v, slot_v, table, table_t, onehot, onehot_own, rank_v,
+    us, ua,
+    ue, ub, tv, dest_v, slot_v, table, table_t, onehot, onehot_own, rank_v,
     matches, picks, chosen, widen, req, req_in, rep, rep_in, dsplit, kv_own, kv, edge_kv, edge_kv_in, kv_halo,
     halo, edge, edge_in, side_raw, side_kv, edge_kv_all, ratio_own, ratio_halo, ratio_side, parts, weights,
     load_sem, tv_sem, req_s, req_r, rep_s, rep_r, row_s, row_r, edge_s, edge_r,
@@ -213,7 +213,7 @@
             )
             for px, py, n, first, count in places
         ]
-        for copy in copies:
+        for copy in copies[2:] + copies[:2]:
             copy.start()
         return copies
 
@@ -225,6 +225,14 @@
     for n in range(2):
         weights[pl.ds(n * CY, CY), pl.ds(0, CY)] = first.astype(BF16)
         weights[pl.ds(n * CY, CY), pl.ds(CY, CY)] = second.astype(BF16)
+
+    def clear(level, carry):
+        for j in range(TR + 1):
+            ue[level, pl.ds(STRIDE * j, 8), :] = jnp.zeros((8, CY), F32)
+            ub[level, pl.ds(STRIDE * j, 8), :] = jnp.zeros((8, CY), F32)
+        return carry
+
+    lax.fori_loop(0, LEV, clear, 0)
 
     pltpu.make_async_copy(req_in.at[pl.ds(0, DEV - 1)], req_in.at[pl.ds(0, DEV - 1)], req_r).wait()
     wanted = req_in[:, 0, :]
@@ -327,6 +335,13 @@
     for i in range(CX // 2):
         assemble(i, 0)
 
+    for g in range(3):
+        acc = jnp.zeros((CX, CY), F32)
+        for m in range(32 if g < 2 else VALS - 64):
+            moved = pltpu.roll(kv[32 * g + m], 4 * m + 2, 1) if 4 * m + 2 < 128 else kv[32 * g + m]
+            acc = jnp.where(lane16 // 4 == m, moved, acc)
+        edge_kv[g] = acc
+    kvedges = to_sides((edge_kv, edge_kv), edge_kv_in, kvedge_s, kvedge_r)
     kvrows = [
         pltpu.make_async_remote_copy(
             kv.at[:, pl.ds(14, 2), :], kv_halo.at[:, pl.ds(6, 2), :],
@@ -339,13 +354,6 @@
     ]
     for copy in kvrows:
         copy.start()
-    for g in range(3):
-        acc = jnp.zeros((CX, CY), F32)
-        for m in range(32 if g < 2 else VALS - 64):
-            moved = pltpu.roll(kv[32 * g + m], 4 * m + 2, 1) if 4 * m + 2 < 128 else kv[32 * g + m]
-            acc = jnp.where(lane16 // 4 == m, moved, acc)
-        edge_kv[g] = acc
-    kvedges = to_sides((edge_kv, edge_kv), edge_kv_in, kvedge_s, kvedge_r)
 
     def factors(before, after, share):
         rest = 1.0 + before * share
@@ -418,8 +426,9 @@
          lambda level, t: ue[level, pl.ds(STRIDE * t + 8, CX), :])
     )
 
+    group = 36
+
     def mix(b, carry):
-        group = 9
         for n in range(group):
             for t in range(TR):
                 at = pl.ds((n * TR + t) * CX, CX)
@@ -432,13 +441,19 @@
                 own = pl.ds(STRIDE * t + 8, CX)
                 at = (n * TR + t) * CX
                 both = mixed[at : at + CX]
-                ua[b * group + n, pl.ds(t * CX, CX), :] = (
-                    ue[b * group + n, own, :] - 0.025 * both[:, :CY]
+                ub[b * group + n, own, :] = both[:, CY:]
+        for n in range(group):
+            for t in range(TR):
+                level, row = b * group + n, STRIDE * t + 8
+                at = (n * TR + t) * CX
+                near = ub[level, pl.ds(row - 1, CX), :] + ub[level, pl.ds(row + 1, CX), :]
+                far = ue[level, pl.ds(row - 2, CX), :] + ue[level, pl.ds(row + 2, CX), :]
+                ua[level, pl.ds(t * CX, CX), :] = ue[level, pl.ds(row, CX), :] - 0.025 * (
+                    (far + near) + mixed[at : at + CX, :CY]
                 )
-                ub[b * group + n, own, :] = both[:, CY:]
-        return carry
-
-    lax.fori_loop(0, LEV // 9, mix, 0)
+        return carry
+
+    lax.fori_loop(0, LEV // group, mix, 0)
 
     for copy in kvrows + kvedges:
         copy.wait_recv()
@@ -488,11 +503,20 @@
         hi, lo = split2(rim)
         parts[pl.ds(level * 2 * TR, 2 * TR), pl.ds(0, CY)] = hi
         parts[pl.ds(level * 2 * TR, 2 * TR), pl.ds(CY, CY)] = lo
-    fixed = jnp.dot(parts[...], weights[:, pl.ds(CY, CY)], preferred_element_type=F32)
+    fixed = jnp.dot(parts[pl.ds(0, LEV * 2 * TR), :], weights[:, pl.ds(CY, CY)], preferred_element_type=F32)
     for level in range(LEV):
         at = level * 2 * TR
-        ub[level, pl.ds(7, TR, stride=STRIDE), :] = fixed[at : at + TR]
-        ub[level, pl.ds(STRIDE, TR, stride=STRIDE), :] = fixed[at + TR : at + 2 * TR]
+        def beside(row):
+            return ue[level, pl.ds(row, TR, stride=STRIDE), :]
+
+        for row, add in (
+            (0, fixed[at : at + TR] + beside(6)),
+            (1, beside(7)),
+            (CX - 2, beside(STRIDE)),
+            (CX - 1, fixed[at + TR : at + 2 * TR] + beside(STRIDE + 1)),
+        ):
+            place = pl.ds(row, TR, stride=CX)
+            ua[level, place, :] = ua[level, place, :] - 0.025 * add
 
     for copy in rows + edges + kvrows + kvedges:
         copy.wait_send()
@@ -500,40 +524,47 @@
     pltpu.make_async_copy(rep.at[pl.ds(0, DEV - 1)], rep.at[pl.ds(0, DEV - 1)], rep_s).wait()
 
 
-def smooth_kernel(ue, us, ua, ub, out, held, side_weights, side_out, sem):
+def smooth_kernel(us, ua, out, held, side_weights, side_out, sem):
     row, col = iota((CY, CY), 0), iota((CY, CY), 1)
     goal = (row % 32) // 16 * 2 + row % 2
     for t in range(TR):
         hit = (row < 64) & ((row % 16) // 2 == t) & (col == (goal + CY - 2) % CY)
         side_weights[:, pl.ds(t * CY, CY)] = jnp.where(hit, 1.0, 0.0).astype(BF16)
 
-    def cells(first):
-        return us[:, pl.ds(first, CX), :].reshape(LEV * CX, CY)
-
-    lane = iota((LEV * CX, CY), 1)
-    u = cells(8)
-    q = 2.0 * (cells(7) + cells(9)) - 8.0 * u
-    across = jnp.where(
-        lane < 16,
-        jnp.where(lane % 2 == 1, pltpu.roll(q, 1, 1), 0.0),
-        jnp.where(lane % 2 == 0, pltpu.roll(q, CY - 1, 1), 0.0),
-    )
-    side = u + across
-    rest = side - side.astype(BF16).astype(F32)
-    both = jnp.where(lane < 32, side, jnp.where(lane < 64, pltpu.roll(rest, 32, 1), 0.0))
-    side_out[...] = jnp.dot(both.astype(BF16), side_weights[...], preferred_element_type=F32)
-
-    count = 9
+    def sides(start, levels):
+        height = levels * CX
+
+        def cells(first):
+            return us[pl.ds(start, levels), pl.ds(first, CX), :].reshape(height, CY)
+
+        lane = iota((height, CY), 1)
+        u = cells(8)
+        q = 2.0 * (cells(7) + cells(9)) - 8.0 * u
+        across = jnp.where(
+            lane < 16,
+            jnp.where(lane % 2 == 1, pltpu.roll(q, 1, 1), 0.0),
+            jnp.where(lane % 2 == 0, pltpu.roll(q, CY - 1, 1), 0.0),
+        )
+        side = u + across
+        rest = side - side.astype(BF16).astype(F32)
+        both = jnp.where(lane < 32, side, jnp.where(lane < 64, pltpu.roll(rest, 32, 1), 0.0))
+        side_out[pl.ds(start * CX, height), :] = jnp.dot(
+            both.astype(BF16), side_weights[...], preferred_element_type=F32
+        )
+
     copies = []
-    for block in range(LEV // count):
-        for level in range(block * count, (block + 1) * count):
+    first = 0
+    for block, count in enumerate((12, 12, 12, 12, 12, 6, 4, 2)):
+        if block == 0:
+            sides(0, count)
+        if block == 1:
+            sides(count, LEV - count)
+        for level in range(first, first + count):
             for t in range(TR):
-                row = STRIDE * t + 8
-                near = ub[level, pl.ds(row - 1, CX), :] + ub[level, pl.ds(row + 1, CX), :]
-                far = ue[level, pl.ds(row - 2, CX), :] + ue[level, pl.ds(row + 2, CX), :]
                 edge = side_out[pl.ds(level * CX, CX), pl.ds(t * CY, CY)]
-                held[t, level] = ua[level, pl.ds(t * CX, CX), :] - 0.025 * ((far + near) + edge)
-        levels = pl.ds(block * count, count)
+                held[t, level] = ua[level, pl.ds(t * CX, CX), :] - 0.025 * edge
+        levels = pl.ds(first, count)
+        first += count
         copy = pltpu.make_async_copy(held.at[:, levels], out.at[:, levels], sem.at[block])
         copy.start()
         copies.append(copy)
@@ -544,17 +575,17 @@
 def local(tracers, group_dest, group_slot, diffusivity, surface_flux):
     any_spec = pl.BlockSpec(memory_space=pltpu.HBM)
     dma = pltpu.SemaphoreType.DMA
-    ue, us, ua, ub = pl.pallas_call(
+    us, ua = pl.pallas_call(
         exchange_kernel,
         out_shape=(
-            pltpu.VMEM((LEV, UROWS, CY), F32),
             pltpu.VMEM((LEV, 32, CY), F32),
             pltpu.VMEM((LEV, TR * CX, CY), F32),
-            pltpu.VMEM((LEV, UROWS, CY), F32),
         ),
         in_specs=[any_spec] * 5,
-        out_specs=(pl.BlockSpec(memory_space=pltpu.VMEM),) * 4,
+        out_specs=(pl.BlockSpec(memory_space=pltpu.VMEM),) * 2,
         scratch_shapes=[
+            pltpu.VMEM((LEV, UROWS, CY), F32),
+            pltpu.VMEM((LEV, UROWS, CY), F32),
             pltpu.VMEM((TR, LEV, CX, CY), F32),
             pltpu.VMEM((CX, CY), jnp.int32),
             pltpu.VMEM((CX, CY), jnp.int32),
@@ -586,14 +617,14 @@
             pltpu.VMEM((LEV, CX, CY), F32),
             pltpu.VMEM((LEV, 8, CY), F32),
             pltpu.VMEM((LEV, 24, CY), F32),
-            pltpu.VMEM((9 * TR * CX, 2 * CY), BF16),
+            pltpu.VMEM((36 * TR * CX, 2 * CY), BF16),
             pltpu.VMEM((2 * CY, 2 * CY), BF16),
             dma((4,)), dma, dma, dma, dma, dma,
             dma((2 * TR,)), dma((2 * TR,)), dma((6,)), dma((6,)),
             dma((2,)), dma((2,)), dma((6,)), dma((6,)),
         ],
         compiler_params=pltpu.CompilerParams(
-            collective_id=0, has_side_effects=True, vmem_limit_bytes=30 << 20
+            collective_id=0, has_side_effects=True, vmem_limit_bytes=48 << 20
         ),
         name="exchange",
     )(
@@ -606,7 +637,7 @@
     return pl.pallas_call(
         smooth_kernel,
         out_shape=jax.ShapeDtypeStruct(tracers.shape, F32),
-        in_specs=[whole] * 4,
+        in_specs=[whole] * 2,
         out_specs=pl.BlockSpec(memory_space=pl.ANY),
         scratch_shapes=[
             pltpu.VMEM((TR, LEV, CX, CY), F32),
@@ -616,7 +647,7 @@
         ],
         compiler_params=pltpu.CompilerParams(vmem_limit_bytes=16 << 20),
         name="smooth",
-    )(ue, us, ua, ub)
+    )(us, ua)
 
 
 def solution(mesh):

time: 37.1 us -> 36.9 us (level)
    pallas_call x1, Pallas kernels: 3.53 us -> 3.02 us  [local(): pl.pallas_call(smooth_kernel, out_shape=jax.ShapeDtypeStruct(tracers.shap...]
where the time goes in v4:
time: 36.9 us; the launch traced here: 36.7 us
  Pallas kernels  36.7 us (99%)
    pallas_call x1, Pallas kernels, local(): pl.pallas_call(exchange_kernel, out_shape=(pltpu.VMEM((LEV, 32, CY), F32)...  33.7 us
    pallas_call x1, Pallas kernels, local(): pl.pallas_call(smooth_kernel, out_shape=jax.ShapeDtypeStruct(tracers.shap...  3.02 us

profile of v4, /device:TPU:1, one launch (start us, length us, event | category | flops | bytes accessed | tf_op | source)
XLA Modules:
  0.0 36.7 jit_solution(2514145672152938043)
XLA Ops:
  0.0 33.7 %exchange.1 = (f32[72,32,128]{2,1,0:T(8,128)S(1)}, f32[72,128,128]{2,1,0:T(8,128)S(1)}) custom-call(f32[8,72,16,128]{3,2,1,0:T(8,128)} %tracers.1, s32[16,128]{1,0:T(8,128)} %dest.1, s32[16,128]{1,0:T(8,128)} %slot.1, f32[72,2048]{1,0:T(8,128)} %diff.1, f32[8,2048]{1,0:T(8,128)} %flux.1), custom_call_target="tpu_custom_call" | custom-call | tf_op jit(solution)/shard_map/exchange/pallas_call | solution.py:578
  33.7 3.0 %smooth.1 = f32[8,72,16,128]{3,2,1,0:T(8,128)} custom-call(f32[72,32,128]{2,1,0:T(8,128)S(1)} %get-tuple-element.7.us, f32[72,128,128]{2,1,0:T(8,128)S(1)} %get-tuple-element.8.ua), custom_call_target="tpu_custom_call" | custom-call | tf_op jit(solution)/shard_map/smooth/pallas_call | solution.py:637

commit v5 on v4

--- a/solution.py
+++ b/solution.py
@@ -455,21 +455,26 @@
 
     lax.fori_loop(0, LEV // group, mix, 0)
 
-    for copy in kvrows + kvedges:
-        copy.wait_recv()
-    for copy in rows:
+    quad = jnp.where(lane24 % 32 < 16, 2, 0) + lane24 % 2
+
+    def spread_kv(rows, index):
+        for level in range(LEV):
+            side_kv[level, rows, :] = jnp.take_along_axis(
+                edge_kv_all[level // 32, rows, :], 4 * (level % 32) + index, axis=1
+            )
+
+    for copy in kvedges[:2]:
         copy.wait_recv()
     for g in range(3):
         edge_kv_all[g, pl.ds(0, CX), :] = jnp.where(lane16 % 4 < 2, edge_kv_in[0, g], edge_kv_in[1, g])
+    spread_kv(pl.ds(0, CX), quad[:CX])
+    for copy in kvrows + kvedges[2:] + rows:
+        copy.wait_recv()
+    for g in range(3):
         over = jnp.where(lane8 % 4 < 2, edge_kv_in[2, g, pl.ds(8, 8)], edge_kv_in[3, g, pl.ds(8, 8)])
         under = jnp.where(lane8 % 4 < 2, edge_kv_in[4, g, pl.ds(0, 8)], edge_kv_in[5, g, pl.ds(0, 8)])
         edge_kv_all[g, pl.ds(CX, 8), :] = jnp.where(sub8 == 7, over, under)
-    quad = jnp.where(lane24 % 32 < 16, 2, 0) + lane24 % 2
-
-    for level in range(LEV):
-        side_kv[level] = jnp.take_along_axis(
-            edge_kv_all[level // 32], 4 * (level % 32) + quad, axis=1
-        )
+    spread_kv(pl.ds(CX, 8), quad[CX:])
 
     side_flux = jnp.take_along_axis(
         edge_kv_all[2], 32 + 4 * ((lane24 % 16) // 2) + quad, axis=1

time: 36.9 us -> 36.6 us (level)
  no operation moved by 1% of the time
where the time goes in v5:
time: 36.6 us; the launch traced here: 36.4 us
  Pallas kernels  36.4 us (99%)
    pallas_call x1, Pallas kernels, local(): pl.pallas_call(exchange_kernel, out_shape=(pltpu.VMEM((LEV, 32, CY), F32)...  33.4 us
    pallas_call x1, Pallas kernels, local(): pl.pallas_call(smooth_kernel, out_shape=jax.ShapeDtypeStruct(tracers.shap...  3.02 us

profile of v5, /device:TPU:1, one launch (start us, length us, event | category | flops | bytes accessed | tf_op | source)
XLA Modules:
  0.0 36.4 jit_solution(5412703462853340392)
XLA Ops:
  0.0 33.4 %exchange.1 = (f32[72,32,128]{2,1,0:T(8,128)S(1)}, f32[72,128,128]{2,1,0:T(8,128)S(1)}) custom-call(f32[8,72,16,128]{3,2,1,0:T(8,128)} %tracers.1, s32[16,128]{1,0:T(8,128)} %dest.1, s32[16,128]{1,0:T(8,128)} %slot.1, f32[72,2048]{1,0:T(8,128)} %diff.1, f32[8,2048]{1,0:T(8,128)} %flux.1), custom_call_target="tpu_custom_call" | custom-call | tf_op jit(solution)/shard_map/exchange/pallas_call | solution.py:583
  33.4 3.0 %smooth.1 = f32[8,72,16,128]{3,2,1,0:T(8,128)} custom-call(f32[72,32,128]{2,1,0:T(8,128)S(1)} %get-tuple-element.7.us, f32[72,128,128]{2,1,0:T(8,128)S(1)} %get-tuple-element.8.ua), custom_call_target="tpu_custom_call" | custom-call | tf_op jit(solution)/shard_map/smooth/pallas_call | solution.py:642
